TPU v7x, 32 devices: a whole 2x2x4 slice. The times are simulated.
32 devices in a mesh: row: 8 (over y, x, core), tensor: 4 (over z).
Axes of the slice: x: 2, y: 2, z: 4, core: 2. Of those that a mesh axis runs over, the one named last changes fastest.
Arguments:
- latents: bfloat16 [4, 16, 64, 2240], P(None, 'row', None, 'tensor'), may hold values from -6 to 6
- clip_height: int32 [4], replicated, may hold values from 8 to 16, as said below
- clip_width: int32 [4], replicated, may hold values from 32 to 64, as said below
- expand_weight: bfloat16 [2, 2240, 5600], P(None, None, 'tensor'), may hold values from -0.125 to 0.125
- expand_bias: float32 [2, 5600], P(None, 'tensor'), may hold values from -3 to 3
- depth_weight: float32 [3, 3, 2, 5600], P(None, None, None, 'tensor'), may hold values from -2 to 2
- depth_bias: float32 [2, 5600], P(None, 'tensor'), may hold values from -3 to 3
- project_weight: bfloat16 [5600, 2240], P('tensor'), may hold values from -0.109375 to 0.109375
Outputs:
- block_output: bfloat16 [4, 16, 64, 2240], P(None, 'row', None, 'tensor')
Inputs may be any that keep to these rules, and one draw needn't show every extreme that they name: `clip_height`: one clip spans all 16 rows and another exactly 8 of them. `clip_width`: one clip spans all 64 columns and another exactly 32 of them.
All inputs are finite; a program needn't handle non-finite values.
Results may differ from a plain program's by a relative error of at most 0.0062.
Values may be sent and summed in bfloat16 or wider, within the bound.
No kernel may reach another device: no remote copies, remote signals or barrier semaphores. Data moves between devices by JAX's collectives and lax.ppermute only.
A program may use at most 128 MiB of HBM per device.

v0:
```python
import functools

import jax
import jax.numpy as jnp
from jax import lax
from jax.experimental import pallas as pl
from jax.experimental.pallas import tpu as pltpu
from jax.sharding import PartitionSpec as P

LANES = 512
GROUP = 16
TILE = 256


def halo_rows(cells):
    count = lax.axis_size("row")
    ends = count - 1
    head = cells[:, :1]
    tail = cells[:, -1:]
    above = lax.ppermute(tail, "row", [(i, i + 1) for i in range(ends)])
    below = lax.ppermute(head, "row", [(i + 1, i) for i in range(ends)])
    return jnp.concatenate([above, cells, below], axis=1)


def depthwise(padded, depth_weight, depth_bias, row_count, col_count):
    widened = jnp.pad(padded, ((0, 0), (0, 0), (1, 1), (0, 0), (0, 0)))
    out_shape = (widened.shape[0], row_count, col_count) + widened.shape[3:]
    depth_out = jnp.zeros(out_shape, jnp.float32) + depth_bias
    for tap_row in range(3):
        for tap_col in range(3):
            depth_out = (
                depth_out
                + depth_weight[tap_row, tap_col]
                * widened[:, tap_row : tap_row + row_count, tap_col : tap_col + col_count]
            )
    return depth_out


def on_device_plain(
    latents,
    clip_height,
    clip_width,
    expand_weight,
    expand_bias,
    depth_weight,
    depth_bias,
    project_weight,
):
    batch_size, row_count, col_count, depth = latents.shape
    tokens = batch_size * row_count * col_count
    first_row = lax.axis_index("row") * row_count
    row_ids = first_row + jnp.arange(row_count, dtype=jnp.int32)
    col_ids = jnp.arange(col_count, dtype=jnp.int32)
    valid_mask = (
        (row_ids[None, :, None] < clip_height[:, None, None])
        & (col_ids[None, None, :] < clip_width[:, None, None])
    ).astype(jnp.float32)[..., None]
    channels = latents.reshape(tokens, depth).T
    gathered = lax.all_gather(channels, "tensor", axis=0, tiled=True)
    pre_act = jnp.einsum("dt,kdf->tkf", gathered, expand_weight, preferred_element_type=jnp.float32)
    pre_act = pre_act.reshape(batch_size, row_count, col_count, 2, -1)
    expanded = (jax.nn.silu(pre_act + expand_bias) * valid_mask[..., None]).astype(jnp.bfloat16)
    padded = halo_rows(expanded)
    depth_out = depthwise(padded, depth_weight, depth_bias, row_count, col_count)
    hidden = (depth_out[:, :, :, 0] * jax.nn.silu(depth_out[:, :, :, 1])).astype(jnp.bfloat16)
    partial_term = jnp.einsum(
        "tf,fd->dt", hidden.reshape(tokens, -1), project_weight, preferred_element_type=jnp.float32
    ).astype(jnp.bfloat16)
    summed = lax.psum_scatter(partial_term, "tensor", scatter_dimension=0, tiled=True)
    summed = summed.T.reshape(latents.shape).astype(jnp.float32)
    return (summed * valid_mask).astype(jnp.bfloat16)


def slot_clips(width_ref, batch_size):
    narrow, least = jnp.int32(0), width_ref[0]
    for b in range(1, batch_size):
        closer = width_ref[b] < least
        narrow = jnp.where(closer, b, narrow)
        least = jnp.where(closer, width_ref[b], least)
    return [jnp.where(narrow <= s, s + 1, s) for s in range(batch_size - 1)] + [narrow]


def slot_widths(batch_size, col_count):
    return [col_count] * (batch_size - 1) + [col_count // 2]


class Chunk:
    def __init__(self, slots, widths, depth):
        self.slots = slots
        self.widths = [widths[s] for s in slots]
        self.starts = [sum(self.widths[:i]) for i in range(len(slots))]
        self.kept = sum(self.widths)
        self.block = -(-self.kept // 128) * 128
        self.depth, self.rest = depth, depth - LANES
        across = LANES // self.block
        groups = self.rest // GROUP
        self.places = [(g // across * GROUP, g % across * self.block) for g in range(groups)]
        self.lines = self.kept + -(-groups // across) * GROUP
        self.tokens = 2 * self.kept
        self.full, self.left = self.tokens // 128, self.tokens % 128
        self.upper = -(-depth // (2 * GROUP)) * GROUP
        self.unit = (self.full * depth + (self.upper if self.left else 0), 128)

    def clips(self, width_ref, batch_size):
        order = slot_clips(width_ref, batch_size)
        return [order[s] for s in self.slots]

    def mask_column(self, height_ref, width_ref, row_id):
        pieces = []
        clips = self.clips(width_ref, width_ref.shape[0])
        for clip, width in zip(clips, self.widths):
            bound = jnp.where((row_id >= 0) & (row_id < height_ref[clip]), width_ref[clip], 0)
            col = lax.broadcasted_iota(jnp.int32, (width, 128), 0)
            pieces.append((col < bound).astype(jnp.float32))
        return jnp.concatenate(pieces, axis=0)

    def put_unit(self, unit_ref, sums):
        depth, at = self.depth, self.full * self.depth
        for b in range(self.full):
            unit_ref[b * depth : (b + 1) * depth, :] = sums[:, b * 128 : (b + 1) * 128]
        if self.left:
            tail = sums[:, self.full * 128 :]
            lower = depth - self.upper
            unit_ref[at : at + self.upper, : self.left] = tail[: self.upper]
            unit_ref[at : at + lower, self.left :] = tail[self.upper :]
            if lower < self.upper:
                unit_ref[at + lower :, self.left :] = jnp.zeros(
                    (self.upper - lower, 128 - self.left), sums.dtype
                )

    def get_unit(self, unit):
        depth, at = self.depth, self.full * self.depth
        blocks = [unit[b * depth : (b + 1) * depth, :] for b in range(self.full)]
        if self.left:
            lower = depth - self.upper
            blocks.append(
                jnp.concatenate(
                    [unit[at : at + self.upper, : self.left], unit[at : at + lower, self.left :]], axis=0
                )
            )
        return jnp.concatenate(blocks, axis=1)


def parity_of():
    return lax.rem(lax.axis_index("row"), 2)


def row_of(place, parity):
    return jnp.where(parity == 0, (-1, 0, 1, 2)[place], (2, 1, 0, -1)[place])


def silu(v):
    h = 0.5 * v
    return h + h * jnp.tanh(h)


def pack_kernel(height_ref, width_ref, x_ref, *refs, chunks):
    parity = parity_of()
    out_refs, mask_refs = refs[: len(chunks)], refs[len(chunks) :]
    for chunk, out_ref, mask_ref in zip(chunks, out_refs, mask_refs):
        for place in range(4):
            row_id = lax.axis_index("row") * 2 + row_of(place, parity)
            mask_ref[place] = chunk.mask_column(height_ref, width_ref, row_id)
        for place in range(2):
            row = jnp.where(parity == 0, 1 - place, place)
            tails = []
            for clip, width, at in zip(
                chunk.clips(width_ref, x_ref.shape[0]), chunk.widths, chunk.starts
            ):
                out_ref[place, at : at + width, :] = x_ref[clip, row, :width, :LANES]
                tails.append(x_ref[clip, row, :width, LANES:].astype(jnp.float32))
            if chunk.block > chunk.kept:
                tails.append(jnp.zeros((chunk.block - chunk.kept, chunk.rest), jnp.float32))
            turned = jnp.concatenate(tails, axis=0).T.astype(jnp.bfloat16)
            kept = chunk.kept
            out_ref[place, kept:, :] = jnp.zeros((chunk.lines - kept, LANES), jnp.bfloat16)
            for g, (down, over) in enumerate(chunk.places):
                out_ref[place, kept + down : kept + down + GROUP, over : over + chunk.block] = turned[
                    g * GROUP : (g + 1) * GROUP
                ]


def tiles_of(hidden_count):
    return [slice(at, min(at + TILE, hidden_count)) for at in range(0, hidden_count, TILE)]


def gather_rows(x_scr, chunk, rows):
    kept = chunk.kept
    for place, packets in enumerate(rows):
        lines = slice(place * kept, (place + 1) * kept)
        tails = []
        for j, packet in enumerate(packets):
            x_scr[lines, j * LANES : (j + 1) * LANES] = packet[:kept, :]
            for down, over in chunk.places:
                tails.append(packet[kept + down : kept + down + GROUP, over : over + chunk.block])
        turned = jnp.concatenate(tails, axis=0).astype(jnp.float32).T
        x_scr[lines, len(packets) * LANES :] = turned[:kept].astype(jnp.bfloat16)


def load_kernel(dw_ref, eb_ref, db_ref, w_ref, out_ref, par_ref, sems, *, shards, depth):
    me = lax.axis_index("tensor")
    rest = depth - LANES
    copies = []
    for k in range(2):
        for j in range(shards):
            base = lax.bitwise_xor(me, j) * depth
            for part, (source, size, target) in enumerate(
                ((base, LANES, j * LANES), (base + LANES, rest, shards * LANES + j * rest))
            ):
                copies.append(
                    pltpu.make_async_copy(
                        w_ref.at[k, pl.ds(pl.multiple_of(source, GROUP), size)],
                        out_ref.at[k, pl.ds(target, size)],
                        sems.at[k, j, part],
                    )
                )
    for copy in copies:
        copy.start()
    for i in range(3):
        for col in range(3):
            par_ref[i * 6 + col * 2 : i * 6 + col * 2 + 2, :] = dw_ref[i, col]
    par_ref[18:20, :] = eb_ref[...]
    par_ref[20:22, :] = db_ref[...]
    for copy in copies:
        copy.wait()


def expand(x_scr, w_ref, par_ref, k, units):
    pre_act = jnp.dot(x_scr[...], w_ref[k, :, units], preferred_element_type=jnp.float32)
    return silu(pre_act + par_ref[18 + k : 19 + k, units])


def masked(cells, mask):
    width = cells.shape[1]
    return cells * jnp.concatenate([mask] * -(-width // 128), axis=1)[:, :width]


def own_kernel(*refs, chunk, shards):
    packet_refs, (mask_ref, par_ref, w_ref, out_ref, x_scr) = refs[:shards], refs[shards:]
    kept = chunk.kept
    gather_rows(x_scr, chunk, [[p.at[1] for p in packet_refs], [p.at[0] for p in packet_refs]])
    mask = jnp.concatenate([mask_ref[1], mask_ref[2]], axis=0)
    for units in tiles_of(w_ref.shape[2]):
        for k in range(2):
            out_ref[k, :, units] = masked(expand(x_scr, w_ref, par_ref, k, units), mask)


def hidden_kernel(*refs, chunk, shards, groups):
    count = len(groups)
    inner_refs, outer_refs = refs[:count], refs[count : 2 * count]
    own_ref, mask_ref, par_ref, w_ref, out_ref, x_scr = refs[2 * count :]
    kept = chunk.kept
    parity = parity_of()
    spots = {j: (g, i) for g, js in enumerate(groups) for i, j in enumerate(js)}
    gather_rows(
        x_scr,
        chunk,
        [[refs_of[spots[j][0]].at[spots[j][1]] for j in range(shards)] for refs_of in (outer_refs, inner_refs)],
    )
    mask = jnp.concatenate([mask_ref[0], mask_ref[3]], axis=0)

    def around(units):
        return [
            masked(expand(x_scr, w_ref, par_ref, k, units), mask) for k in range(2)
        ]

    def convolve(units, cells):
        width = units.stop - units.start
        line = lax.broadcasted_iota(jnp.int32, (kept, width), 0)
        not_first, not_last = None, None
        for at, size in zip(chunk.starts, chunk.widths):
            first, last = line != at, line != at + size - 1
            not_first = first if not_first is None else not_first & first
            not_last = last if not_last is None else not_last & last
        halves = ([], [])
        for k in range(2):
            rows = [
                cells[k][:kept],
                own_ref[k, :kept, units],
                own_ref[k, kept:, units],
                cells[k][kept:],
            ]
            taps = [
                [
                    jnp.where(
                        parity == 0,
                        par_ref[i * 6 + col * 2 + k : i * 6 + col * 2 + k + 1, units],
                        par_ref[(2 - i) * 6 + col * 2 + k : (2 - i) * 6 + col * 2 + k + 1, units],
                    )
                    for col in range(3)
                ]
                for i in range(3)
            ]
            for place in range(2):
                sums = []
                for tap_col in range(3):
                    total = None
                    for i in range(3):
                        term = taps[i][tap_col] * rows[place + i]
                        total = term if total is None else total + term
                    sums.append(total)
                left = jnp.where(not_first, pltpu.roll(sums[0], 1, 0), 0.0)
                right = jnp.where(not_last, pltpu.roll(sums[2], kept - 1, 0), 0.0)
                halves[k].append(sums[1] + left + right + par_ref[20 + k : 21 + k, units])
        for place in range(2):
            hidden = halves[0][place] * silu(halves[1][place])
            out_ref[(1 - place) * kept : (2 - place) * kept, units] = hidden.astype(jnp.bfloat16)

    tiles = tiles_of(w_ref.shape[2])
    cells = around(tiles[0])
    for t, units in enumerate(tiles):
        coming = around(tiles[t + 1]) if t + 1 < len(tiles) else None
        convolve(units, cells)
        cells = coming


def project(weight_ref, hidden_ref, depth, j):
    start = lax.bitwise_xor(lax.axis_index("tensor"), j) * depth
    return lax.dot_general(
        weight_ref[pl.ds(pl.multiple_of(start, GROUP), depth), :],
        hidden_ref[...],
        (((1,), (1,)), ((), ())),
        preferred_element_type=jnp.float32,
    )


def unit_kernel(weight_ref, hidden_ref, *refs, chunk, j):
    out_ref = refs[-1]
    sums = project(weight_ref, hidden_ref, chunk.depth, j)
    for ref in refs[:-1]:
        sums = sums + chunk.get_unit(ref[...].astype(jnp.float32))
    chunk.put_unit(out_ref, sums.astype(jnp.bfloat16))


def final_kernel(width_ref, mask_ref, weight_ref, hidden_ref, *refs, chunk, sources):
    out_ref = refs[-1]
    if len(refs) > sources + 1:
        out_ref[...] = refs[sources][...]
    sums = project(weight_ref, hidden_ref, chunk.depth, 0)
    for ref in refs[:sources]:
        sums = sums + chunk.get_unit(ref[...].astype(jnp.float32))
    cells = sums.T
    parity = parity_of()
    for place in range(2):
        row = jnp.where(parity == 0, 1 - place, place)
        mask = mask_ref[2 - place][:, :1] > 0
        part = cells[place * chunk.kept : (place + 1) * chunk.kept]
        part = jnp.where(mask, part, 0.0).astype(jnp.bfloat16)
        clips = chunk.clips(width_ref, width_ref.shape[0])
        for clip, width, at in zip(clips, chunk.widths, chunk.starts):
            out_ref[clip, row, :width, :] = part[at : at + width]
            if width < out_ref.shape[2]:
                blank = jnp.zeros((out_ref.shape[2] - width, chunk.depth), jnp.bfloat16)
                out_ref[clip, row, width:, :] = blank


VMEM = pl.BlockSpec(memory_space=pltpu.VMEM)
MIB = 1024 * 1024


def after(value, *others):
    return lax.optimization_barrier((value,) + others)[0]


def on_device_packed(
    latents,
    clip_height,
    clip_width,
    expand_weight,
    expand_bias,
    depth_weight,
    depth_bias,
    project_weight,
):
    batch_size, row_count, col_count, depth = latents.shape
    shards, row_devices = lax.axis_size("tensor"), lax.axis_size("row")
    hidden_count = expand_weight.shape[2]
    full_depth = shards * depth
    chunks = chunks_of(batch_size, col_count, depth)
    count = len(chunks)
    packed = pl.pallas_call(
        functools.partial(pack_kernel, chunks=chunks),
        out_shape=[jax.ShapeDtypeStruct((2, c.lines, LANES), jnp.bfloat16) for c in chunks]
        + [jax.ShapeDtypeStruct((4, c.kept, 128), jnp.float32) for c in chunks],
        grid_spec=pltpu.PrefetchScalarGridSpec(
            num_scalar_prefetch=2, grid=(), in_specs=[VMEM], out_specs=[VMEM] * (2 * count)
        ),
        compiler_params=pltpu.CompilerParams(vmem_limit_bytes=16 * MIB),
        name="pack",
    )(clip_height, clip_width, latents)
    own, masks = packed[:count], packed[count:]
    project_turned = project_weight.T

    sibling = [(i, i ^ 1) for i in range(row_devices)]
    beyond = [(i, i + 1) for i in range(1, row_devices - 1, 2)]
    beyond = beyond + [(b, a) for a, b in beyond]
    near = [(i, i ^ 1) for i in range(4)]
    two_off = [(i, i ^ 2) for i in range(4)]
    middle = [(1, 2), (2, 1)]
    to_end = [(2, 3), (1, 0)]
    from_end = [(0, 1), (3, 2)]

    def edge_rows(packets, groups):
        return [
            [jnp.concatenate([packets[j][side : side + 1] for j in js], axis=0) for js in groups]
            for side in range(2)
        ]

    def send_rows(inner, outer):
        return (
            [lax.ppermute(x, "row", sibling) for x in inner],
            [lax.ppermute(x, "row", beyond) for x in outer],
        )

    def relay(mine, *others):
        second = lax.ppermute(mine, "tensor", two_off)
        first = lax.ppermute(mine, "tensor", near)
        across = lax.ppermute(after(mine, second, *others), "tensor", middle)
        passed = lax.ppermute(after(second, *others), "tensor", to_end)
        return [mine, first, second, across + passed]

    def direct(mine):
        return [mine] + [
            lax.ppermute(mine, "tensor", [(i, i ^ j) for i in range(4)]) for j in range(1, 4)
        ]

    out = None
    weights, parameters = pl.pallas_call(
        functools.partial(load_kernel, shards=shards, depth=depth),
        out_shape=[
            jax.ShapeDtypeStruct(expand_weight.shape, jnp.bfloat16),
            jax.ShapeDtypeStruct((22, hidden_count), jnp.float32),
        ],
        in_specs=[VMEM] * 3 + [pl.BlockSpec(memory_space=pl.ANY)],
        out_specs=[VMEM, VMEM],
        scratch_shapes=[pltpu.SemaphoreType.DMA((2, shards, 2))],
        compiler_params=pltpu.CompilerParams(vmem_limit_bytes=36 * MIB),
        name="load_weights",
    )(depth_weight, expand_bias, depth_bias, after(expand_weight, own[0]))
    groups = ((0,), (1, 2), (3,))
    inner, outer = send_rows(*edge_rows(own[:1], groups[:1]))
    packets = relay(own[0], parameters, *inner, *outer)
    edges = edge_rows(packets, groups[1:])
    later = send_rows(*edges)
    inner, outer = inner + later[0], outer + later[1]
    upcoming = direct(after(own[1], edges[0][-1], edges[1][-1]))
    for number, chunk in enumerate(chunks):
        if number:
            packets, groups = list(lax.optimization_barrier((*upcoming, hidden))[:shards]), ((0, 1, 2, 3),)
            inner, outer = send_rows(*edge_rows(packets, groups))
            packets[0] = after(packets[0], far)
        rows = pl.pallas_call(
            functools.partial(own_kernel, chunk=chunk, shards=shards),
            out_shape=jax.ShapeDtypeStruct((2, chunk.tokens, hidden_count), jnp.float32),
            in_specs=[VMEM] * (shards + 3),
            out_specs=VMEM,
            scratch_shapes=[pltpu.VMEM((chunk.tokens, full_depth), jnp.bfloat16)],
            compiler_params=pltpu.CompilerParams(vmem_limit_bytes=16 * MIB),
            cost_estimate=pl.CostEstimate(
                flops=1000,
                bytes_accessed=1000,
                transcendentals=0,
            ),
            name="expand_own",
        )(*packets, masks[number], parameters, weights)
        if number:
            inner[0] = after(inner[0], last_unit)
        hidden = pl.pallas_call(
            functools.partial(hidden_kernel, chunk=chunk, shards=shards, groups=groups),
            out_shape=jax.ShapeDtypeStruct((chunk.tokens, hidden_count), jnp.bfloat16),
            in_specs=[VMEM] * (2 * len(groups) + 4),
            out_specs=VMEM,
            scratch_shapes=[pltpu.VMEM((chunk.tokens, full_depth), jnp.bfloat16)],
            compiler_params=pltpu.CompilerParams(vmem_limit_bytes=16 * MIB),
            cost_estimate=pl.CostEstimate(
                flops=1000,
                bytes_accessed=1000,
                transcendentals=0,
            ),
            name="expand_conv",
        )(*inner, *outer, rows, masks[number], parameters, weights)

        cost = pl.CostEstimate(
            flops=2 * chunk.tokens * depth * hidden_count,
            bytes_accessed=2 * depth * hidden_count + 2 * chunk.tokens * hidden_count,
            transcendentals=0,
        )

        def unit(j, *added):
            return pl.pallas_call(
                functools.partial(unit_kernel, chunk=chunk, j=j),
                out_shape=jax.ShapeDtypeStruct(chunk.unit, jnp.bfloat16),
                in_specs=[VMEM] * (2 + len(added)),
                out_specs=VMEM,
                compiler_params=pltpu.CompilerParams(vmem_limit_bytes=16 * MIB),
                cost_estimate=cost,
                name=f"project_{j}",
            )(project_turned, hidden, *added)

        if number:
            hidden = after(hidden, *arrived)
        far = unit(3)
        relayed = lax.ppermute(far, "tensor", from_end)
        across = lax.ppermute(far, "tensor", middle)
        close = unit(1)
        relayed, across = lax.optimization_barrier((relayed, across))
        last_unit = unit(2, relayed)
        arrived = [
            across,
            lax.ppermute(last_unit, "tensor", two_off),
            lax.ppermute(after(close, relayed), "tensor", near),
        ]
        extra = [] if out is None else [out]
        out = pl.pallas_call(
            functools.partial(final_kernel, chunk=chunk, sources=len(arrived)),
            out_shape=jax.ShapeDtypeStruct(latents.shape, jnp.bfloat16),
            grid_spec=pltpu.PrefetchScalarGridSpec(
                num_scalar_prefetch=1,
                grid=(),
                in_specs=[VMEM] * (3 + len(arrived) + len(extra)),
                out_specs=VMEM,
            ),
            compiler_params=pltpu.CompilerParams(vmem_limit_bytes=16 * MIB),
            cost_estimate=cost,
            name="finish",
        )(clip_width, masks[number], project_turned, hidden, *arrived, *extra)
    return out


def chunks_of(batch_size, col_count, depth):
    widths = slot_widths(batch_size, col_count)
    half = batch_size // 2
    return [Chunk(slots, widths, depth) for slots in (list(range(half)), list(range(half, batch_size)))]


def on_device(latents, clip_height, clip_width, expand_weight, *rest_of):
    batch_size, row_count, col_count, depth = latents.shape
    fits = (
        batch_size >= 2
        and row_count == 2
        and lax.axis_size("row") % 2 == 0
        and lax.axis_size("tensor") == 4
        and depth > LANES
        and (depth - LANES) % GROUP == 0
        and depth % GROUP == 0
        and all(
            c.block in (128, 256, 512) and c.kept % GROUP == 0 and c.left in (0, 64)
            for c in chunks_of(batch_size, col_count, depth)
        )
    )
    run = on_device_packed if fits else on_device_plain
    return run(latents, clip_height, clip_width, expand_weight, *rest_of)


def solution(mesh):
    in_specs = (
        P(None, "row", None, "tensor"),
        P(),
        P(),
        P(None, None, "tensor"),
        P(None, "tensor"),
        P(None, None, None, "tensor"),
        P(None, "tensor"),
        P("tensor", None),
    )
    out_specs = P(None, "row", None, "tensor")
    return jax.shard_map(
        on_device, mesh=mesh, in_specs=in_specs, out_specs=out_specs, check_vma=False
    )
```

profile of v0, /device:TPU:2, one launch (start us, length us, event | category | flops | bytes accessed | tf_op | source)
XLA Modules:
  0.0 105.9 jit_solution(3958214290792103811)
XLA Ops:
  0.0 1.1 %copy-done = bf16[4,2,64,560]{3,2,1,0:T(8,128)(2,1)S(1)} copy-done((bf16[4,2,64,560]{3,2,1,0:T(8,128)(2,1)S(1)}, bf16[4,2,64,560]{3,2,1,0:T(8,128)(2,1)}, u32[]{:S(2)}) %copy-start) | copy-done | bytes 573464
  1.1 0.7 copy-done.4
  1.7 0.7 copy-done.6
  2.4 0.7 pack.1
  3.1 2.7 %collective-permute-start = (bf16[2,144,512]{2,1,0:T(8,128)(2,1)S(1)}, bf16[2,144,512]{2,1,0:T(8,128)(2,1)S(1)}, u32[]{:S(2)}, u32[]{:S(2)}) collective-permute-start(bf16[2,144,512]{2,1,0:T(8,128)(2,1)S(1)} %get-tuple-element.33.refs_0_), channel_id=1, source_target_pairs={{0,2},{1,3},{2,0},{3,1},{4,6},{5,7},{6,4},{7,5},{8,10},{9,11},{10,... | collective-permute-start | bytes 884744 | tf_op jit(solution)/shard_map/ppermute | solution.py:416
  5.8 0.1 collective-permute-start.1
  5.9 2.5 %collective-permute-start.2 = (bf16[1,144,512]{2,1,0:T(8,128)(2,1)S(1)}, bf16[1,144,512]{2,1,0:T(8,128)(2,1)S(1)}, u32[]{:S(2)}, u32[]{:S(2)}) collective-permute-start(bf16[1,144,512]{2,1,0:T(8,128)(2,1)S(1)} %get-tuple-element.57), channel_id=1, source_target_pairs={{4,8},{12,16},{20,24},{8,4},{16,12},{24,20},{5,9},{13,17},{21,25},... | collective-permute-start | bytes 442376 | tf_op jit(solution)/shard_map/ppermute | solution.py:412
  8.4 1.6 %collective-permute-start.8 = (bf16[2,144,512]{2,1,0:T(8,128)(2,1)S(1)}, bf16[2,144,512]{2,1,0:T(8,128)(2,1)S(1)}, u32[]{:S(2)}, u32[]{:S(2)}) collective-permute-start(bf16[2,144,512]{2,1,0:T(8,128)(2,1)S(1)} %get-tuple-element.33.refs_0_), channel_id=1, source_target_pairs={{0,1},{1,0},{2,3},{3,2},{4,5},{5,4},{6,7},{7,6},{8,9},{9,8},{10,11... | collective-permute-start | bytes 884744 | tf_op jit(solution)/shard_map/ppermute | solution.py:417
  10.0 0.9 copy-done.1
  10.9 0.7 copy-done.2
  11.6 0.7 copy-done.3
  12.3 4.8 %load_weights.1 = (bf16[2,2240,1400]{2,1,0:T(8,128)(2,1)S(1)}, f32[22,1400]{1,0:T(8,128)S(1)}) custom-call(f32[3,3,2,1400]{3,2,1,0:T(2,128)S(1)} %copy-done.1, f32[2,1400]{1,0:T(2,128)S(1)} %copy-done.2, f32[2,1400]{1,0:T(2,128)S(1)} %copy-done.3, bf16[2,2240,1400]{2,1,0:T(8,128)(2,1)} %w_ref), custom_call_target="tpu_custom_call" | custom-call | tf_op jit(solution)/shard_map/load_weights/pallas_call | solution.py:428
  17.1 2.1 %collective-permute-done.refs_2_ = bf16[2,144,512]{2,1,0:T(8,128)(2,1)S(1)} collective-permute-done((bf16[2,144,512]{2,1,0:T(8,128)(2,1)S(1)}, bf16[2,144,512]{2,1,0:T(8,128)(2,1)S(1)}, u32[]{:S(2)}, u32[]{:S(2)}) %collective-permute-start) | collective-permute-done | bytes 294944 | tf_op jit(solution)/shard_map/ppermute | solution.py:416
  19.2 0.7 collective-permute-start.3
  19.9 1.3 %collective-permute-start.4 = (bf16[2,144,512]{2,1,0:T(8,128)(2,1)S(1)}, bf16[2,144,512]{2,1,0:T(8,128)(2,1)S(1)}, u32[]{:S(2)}, u32[]{:S(2)}) collective-permute-start(bf16[2,144,512]{2,1,0:T(8,128)(2,1)S(1)} %collective-permute-done.refs_2_), channel_id=1, source_target_pairs={{2,3},{1,0},{6,7},{5,4},{10,11},{9,8},{14,15},{13,12},{18,19},{17,... | collective-permute-start | bytes 884744 | tf_op jit(solution)/shard_map/ppermute | solution.py:419
  21.2 2.3 %collective-permute-done.8.refs_1_ = bf16[2,144,512]{2,1,0:T(8,128)(2,1)S(1)} collective-permute-done((bf16[2,144,512]{2,1,0:T(8,128)(2,1)S(1)}, bf16[2,144,512]{2,1,0:T(8,128)(2,1)S(1)}, u32[]{:S(2)}, u32[]{:S(2)}) %collective-permute-start.8) | collective-permute-done | bytes 294944 | tf_op jit(solution)/shard_map/ppermute | solution.py:417
  23.6 1.9 %collective-permute-start.11 = (bf16[2,144,512]{2,1,0:T(8,128)(2,1)S(1)}, bf16[2,144,512]{2,1,0:T(8,128)(2,1)S(1)}, u32[]{:S(2)}, u32[]{:S(2)}) collective-permute-start(bf16[2,144,512]{2,1,0:T(8,128)(2,1)S(1)} %pad_maximum_fusion.3), channel_id=1, source_target_pairs={{4,8},{12,16},{20,24},{8,4},{16,12},{24,20},{5,9},{13,17},{21,25},... | collective-permute-start | bytes 884744 | tf_op jit(solution)/shard_map/ppermute | solution.py:412
  25.6 1.7 %collective-permute-start.9 = (bf16[2,144,512]{2,1,0:T(8,128)(2,1)S(1)}, bf16[2,144,512]{2,1,0:T(8,128)(2,1)S(1)}, u32[]{:S(2)}, u32[]{:S(2)}) collective-permute-start(bf16[2,144,512]{2,1,0:T(8,128)(2,1)S(1)} %pad_maximum_fusion.2), channel_id=1, source_target_pairs={{0,4},{4,0},{8,12},{12,8},{16,20},{20,16},{24,28},{28,24},{1,5},{5... | collective-permute-start | bytes 884744 | tf_op jit(solution)/shard_map/ppermute | solution.py:411
  27.3 3.0 %collective-permute-done.4 = bf16[2,144,512]{2,1,0:T(8,128)(2,1)S(1)} collective-permute-done((bf16[2,144,512]{2,1,0:T(8,128)(2,1)S(1)}, bf16[2,144,512]{2,1,0:T(8,128)(2,1)S(1)}, u32[]{:S(2)}, u32[]{:S(2)}) %collective-permute-start.4) | collective-permute-done | bytes 294944 | tf_op jit(solution)/shard_map/ppermute | solution.py:419
  30.2 0.1 add.3.refs_3_
  30.3 0.5 collective-permute-start.5
  30.8 4.1 %collective-permute-start.6 = (bf16[2,112,512]{2,1,0:T(8,128)(2,1)S(1)}, bf16[2,112,512]{2,1,0:T(8,128)(2,1)S(1)}, u32[]{:S(2)}, u32[]{:S(2)}) collective-permute-start(bf16[2,112,512]{2,1,0:T(8,128)(2,1)S(1)} %get-tuple-element.44.refs_0_), channel_id=1, source_target_pairs={{0,2},{1,3},{2,0},{3,1},{4,6},{5,7},{6,4},{7,5},{8,10},{9,11},{10,... | collective-permute-start | bytes 688136 | tf_op jit(solution)/shard_map/ppermute | solution.py:424
  34.9 2.5 %collective-permute-start.12 = (bf16[1,144,512]{2,1,0:T(8,128)(2,1)S(1)}, bf16[1,144,512]{2,1,0:T(8,128)(2,1)S(1)}, u32[]{:S(2)}, u32[]{:S(2)}) collective-permute-start(bf16[1,144,512]{2,1,0:T(8,128)(2,1)S(1)} %get-tuple-element.55), channel_id=1, source_target_pairs={{4,8},{12,16},{20,24},{8,4},{16,12},{24,20},{5,9},{13,17},{21,25},... | collective-permute-start | bytes 442376 | tf_op jit(solution)/shard_map/ppermute | solution.py:412
  37.5 4.0 %expand_own.2.refs_6_ = f32[2,256,1400]{2,1,0:T(8,128)S(1)} custom-call(bf16[2,144,512]{2,1,0:T(8,128)(2,1)S(1)} %get-tuple-element.33.refs_0_, bf16[2,144,512]{2,1,0:T(8,128)(2,1)S(1)} %collective-permute-done.8.refs_1_, bf16[2,144,512]{2,1,0:T(8,128)(2,1)S(1)} %collective-permute-done.refs_2_, bf16[2,144,512]{2,1,0:T(8,128)(2,1)S(1)} %add.3.refs_3_, ...), custom_call_target="tpu_custom_call" | custom-call | flops 1000 | bytes 1000 | tf_op jit(solution)/shard_map/expand_own/pallas_call | solution.py:452
  41.5 6.7 %expand_conv.2.hidden_ref = bf16[256,1400]{1,0:T(8,128)(2,1)S(1)} custom-call(bf16[1,144,512]{2,1,0:T(8,128)(2,1)S(1)} %collective-permute-done.1.refs_0_, bf16[2,144,512]{2,1,0:T(8,128)(2,1)S(1)} %collective-permute-done.9.refs_1_, bf16[1,144,512]{2,1,0:T(8,128)(2,1)S(1)} %collective-permute-done.10.refs_2_, ...), custom_call_target="tpu_custom_call" | custom-call | flops 1000 | bytes 1000 | tf_op jit(solution)/shard_map/expand_conv/pallas_call | solution.py:468
  48.2 0.6 project_3.2
  48.9 2.5 %collective-permute-start.14 = (bf16[1120,128]{1,0:T(8,128)(2,1)S(1)}, bf16[1120,128]{1,0:T(8,128)(2,1)S(1)}, u32[]{:S(2)}, u32[]{:S(2)}) collective-permute-start(bf16[1120,128]{1,0:T(8,128)(2,1)S(1)} %project_3.2), channel_id=1, source_target_pairs={{0,1},{3,2},{4,5},{7,6},{8,9},{11,10},{12,13},{15,14},{16,17},{19,... | collective-permute-start | bytes 860168 | tf_op jit(solution)/shard_map/ppermute | solution.py:503
  51.4 0.7 collective-permute-start.15
  52.2 2.3 %collective-permute-start.13 = (bf16[4,112,512]{2,1,0:T(8,128)(2,1)S(1)}, bf16[4,112,512]{2,1,0:T(8,128)(2,1)S(1)}, u32[]{:S(2)}, u32[]{:S(2)}) collective-permute-start(bf16[4,112,512]{2,1,0:T(8,128)(2,1)S(1)} %pad_maximum_fusion), channel_id=1, source_target_pairs={{0,4},{4,0},{8,12},{12,8},{16,20},{20,16},{24,28},{28,24},{1,5},{5... | collective-permute-start | bytes 1376264 | tf_op jit(solution)/shard_map/ppermute | solution.py:411
  54.6 2.1 %collective-permute-start.16 = (bf16[4,112,512]{2,1,0:T(8,128)(2,1)S(1)}, bf16[4,112,512]{2,1,0:T(8,128)(2,1)S(1)}, u32[]{:S(2)}, u32[]{:S(2)}) collective-permute-start(bf16[4,112,512]{2,1,0:T(8,128)(2,1)S(1)} %pad_maximum_fusion.1), channel_id=1, source_target_pairs={{4,8},{12,16},{20,24},{8,4},{16,12},{24,20},{5,9},{13,17},{21,25},... | collective-permute-start | bytes 1376264 | tf_op jit(solution)/shard_map/ppermute | solution.py:412
  56.7 0.6 project_1.2
  57.4 0.6 project_2.2
  58.1 4.4 %collective-permute-start.18 = (bf16[1120,128]{1,0:T(8,128)(2,1)S(1)}, bf16[1120,128]{1,0:T(8,128)(2,1)S(1)}, u32[]{:S(2)}, u32[]{:S(2)}) collective-permute-start(bf16[1120,128]{1,0:T(8,128)(2,1)S(1)} %project_1.2), channel_id=1, source_target_pairs={{0,1},{1,0},{2,3},{3,2},{4,5},{5,4},{6,7},{7,6},{8,9},{9,8},{10,11... | collective-permute-start | bytes 860168 | tf_op jit(solution)/shard_map/ppermute | solution.py:511
  62.5 1.8 %collective-permute-start.17 = (bf16[1120,128]{1,0:T(8,128)(2,1)S(1)}, bf16[1120,128]{1,0:T(8,128)(2,1)S(1)}, u32[]{:S(2)}, u32[]{:S(2)}) collective-permute-start(bf16[1120,128]{1,0:T(8,128)(2,1)S(1)} %project_2.2), channel_id=1, source_target_pairs={{0,2},{1,3},{2,0},{3,1},{4,6},{5,7},{6,4},{7,5},{8,10},{9,11},{10,... | collective-permute-start | bytes 860168 | tf_op jit(solution)/shard_map/ppermute | solution.py:510
  64.3 3.0 %expand_own.3.refs_2_ = f32[2,192,1400]{2,1,0:T(8,128)S(1)} custom-call(bf16[2,112,512]{2,1,0:T(8,128)(2,1)S(1)} %get-tuple-element.44.refs_0_, bf16[2,112,512]{2,1,0:T(8,128)(2,1)S(1)} %collective-permute-done.5.refs_1_, bf16[2,112,512]{2,1,0:T(8,128)(2,1)S(1)} %collective-permute-done.6.refs_2_, bf16[2,112,512]{2,1,0:T(8,128)(2,1)S(1)} %collective-permute-done.7.refs_3_, ...), custom_call_target="tpu_custom_call" | custom-call | flops 1000 | bytes 1000 | tf_op jit(solution)/shard_map/expand_own/pallas_call | solution.py:452
  67.3 5.1 %expand_conv.3.hidden_ref = bf16[192,1400]{1,0:T(8,128)(2,1)S(1)} custom-call(bf16[4,112,512]{2,1,0:T(8,128)(2,1)S(1)} %collective-permute-done.13.refs_0_, bf16[4,112,512]{2,1,0:T(8,128)(2,1)S(1)} %collective-permute-done.16.refs_1_, f32[2,192,1400]{2,1,0:T(8,128)S(1)} %expand_own.3.refs_2_, f32[4,96,128]{2,1,0:T(8,128)S(1)} %get-tuple-element.28.refs_4_.refs_3_.mask_ref, ...), custom_call_target="tpu_custom_call" | custom-call | flops 1000 | bytes 1000 | tf_op jit(solution)/shard_map/expand_conv/pallas_call | solution.py:468
  72.4 3.4 %collective-permute-done.18.refs_2_ = bf16[1120,128]{1,0:T(8,128)(2,1)S(1)} collective-permute-done((bf16[1120,128]{1,0:T(8,128)(2,1)S(1)}, bf16[1120,128]{1,0:T(8,128)(2,1)S(1)}, u32[]{:S(2)}, u32[]{:S(2)}) %collective-permute-start.18) | collective-permute-done | bytes 286752 | tf_op jit(solution)/shard_map/ppermute | solution.py:511
  75.8 0.7 project_3.3
  76.5 6.1 %collective-permute-start.19 = (bf16[848,128]{1,0:T(8,128)(2,1)S(1)}, bf16[848,128]{1,0:T(8,128)(2,1)S(1)}, u32[]{:S(2)}, u32[]{:S(2)}) collective-permute-start(bf16[848,128]{1,0:T(8,128)(2,1)S(1)} %project_3.3), channel_id=1, source_target_pairs={{0,1},{3,2},{4,5},{7,6},{8,9},{11,10},{12,13},{15,14},{16,17},{19,... | collective-permute-start | bytes 651272 | tf_op jit(solution)/shard_map/ppermute | solution.py:503
  82.7 0.7 collective-permute-start.20
  83.3 0.7 project_1.3
  84.0 3.4 %collective-permute-done.19.refs_0_ = bf16[848,128]{1,0:T(8,128)(2,1)S(1)} collective-permute-done((bf16[848,128]{1,0:T(8,128)(2,1)S(1)}, bf16[848,128]{1,0:T(8,128)(2,1)S(1)}, u32[]{:S(2)}, u32[]{:S(2)}) %collective-permute-start.19) | collective-permute-done | bytes 217120 | tf_op jit(solution)/shard_map/ppermute | solution.py:503
  87.5 0.7 project_2.3
  88.1 3.8 %collective-permute-start.22 = (bf16[848,128]{1,0:T(8,128)(2,1)S(1)}, bf16[848,128]{1,0:T(8,128)(2,1)S(1)}, u32[]{:S(2)}, u32[]{:S(2)}) collective-permute-start(bf16[848,128]{1,0:T(8,128)(2,1)S(1)} %project_1.3), channel_id=1, source_target_pairs={{0,1},{1,0},{2,3},{3,2},{4,5},{5,4},{6,7},{7,6},{8,9},{9,8},{10,11... | collective-permute-start | bytes 651272 | tf_op jit(solution)/shard_map/ppermute | solution.py:511
  92.0 1.3 %finish.2.refs_3_ = bf16[4,2,64,560]{3,2,1,0:T(8,128)(2,1)S(1)} custom-call(s32[4]{0:T(128)S(1)} %copy-done.5, f32[4,128,128]{2,1,0:T(8,128)S(1)} %get-tuple-element.36.refs_4_.refs_7_.mask_ref, bf16[2240,1400]{1,0:T(8,128)(2,1)S(1)} %bitcast.9, bf16[256,1400]{1,0:T(8,128)(2,1)S(1)} %expand_conv.2.hidden_ref, ...), custom_call_target="tpu_custom_call" | custom-call | flops 401408000 | bytes 2284800 | tf_op jit(solution)/shard_map/finish/pallas_call | solution.py:514
  93.3 6.9 %collective-permute-done.22.refs_2_ = bf16[848,128]{1,0:T(8,128)(2,1)S(1)} collective-permute-done((bf16[848,128]{1,0:T(8,128)(2,1)S(1)}, bf16[848,128]{1,0:T(8,128)(2,1)S(1)}, u32[]{:S(2)}, u32[]{:S(2)}) %collective-permute-start.22) | collective-permute-done | bytes 217120 | tf_op jit(solution)/shard_map/ppermute | solution.py:511
  100.3 3.5 %collective-permute-done.21.refs_1_ = bf16[848,128]{1,0:T(8,128)(2,1)S(1)} collective-permute-done((bf16[848,128]{1,0:T(8,128)(2,1)S(1)}, bf16[848,128]{1,0:T(8,128)(2,1)S(1)}, u32[]{:S(2)}, u32[]{:S(2)}) %collective-permute-start.21) | collective-permute-done | bytes 217120 | tf_op jit(solution)/shard_map/ppermute | solution.py:510
  103.8 2.2 %finish.3 = bf16[4,2,64,560]{3,2,1,0:T(8,128)(2,1)} custom-call(s32[4]{0:T(128)S(1)} %copy-done.5, f32[4,96,128]{2,1,0:T(8,128)S(1)} %get-tuple-element.28.refs_4_.refs_3_.mask_ref, bf16[2240,1400]{1,0:T(8,128)(2,1)S(1)} %bitcast.10, bf16[192,1400]{1,0:T(8,128)(2,1)S(1)} %expand_conv.3.hidden_ref, bf16[848,128]{1,0:T(8,128)(2,1)S(1)} %collective-permute-done.20.refs_0_, ...), custom_call_target="tpu_custom_call" | custom-call | flops 301056000 | bytes 2105600 | tf_op jit(solution)/shard_map/finish/pallas_call | solution.py:514
  (42 shorter events, 0.4 us)
Async XLA Ops:
  0.0 1.1 %copy-start = (bf16[4,2,64,560]{3,2,1,0:T(8,128)(2,1)S(1)}, bf16[4,2,64,560]{3,2,1,0:T(8,128)(2,1)}, u32[]{:S(2)}) copy-start(bf16[4,2,64,560]{3,2,1,0:T(8,128)(2,1)} %x_ref.1) | copy-start | bytes 1720324
  1.1 0.7 copy-start.4
  1.7 0.7 copy-start.6
  3.1 16.1 %collective-permute-start = (bf16[2,144,512]{2,1,0:T(8,128)(2,1)S(1)}, bf16[2,144,512]{2,1,0:T(8,128)(2,1)S(1)}, u32[]{:S(2)}, u32[]{:S(2)}) collective-permute-start(bf16[2,144,512]{2,1,0:T(8,128)(2,1)S(1)} %get-tuple-element.33.refs_0_), channel_id=1, source_target_pairs={{0,2},{1,3},{2,0},{3,1},{4,6},{5,7},{6,4},{7,5},{8,10},{9,11},{10,... | collective-permute-start | bytes 884744 | tf_op jit(solution)/shard_map/ppermute | solution.py:416
  5.8 11.3 %collective-permute-start.1 = (bf16[1,144,512]{2,1,0:T(8,128)(2,1)S(1)}, bf16[1,144,512]{2,1,0:T(8,128)(2,1)S(1)}, u32[]{:S(2)}, u32[]{:S(2)}) collective-permute-start(bf16[1,144,512]{2,1,0:T(8,128)(2,1)S(1)} %get-tuple-element.58), channel_id=1, source_target_pairs={{0,4},{4,0},{8,12},{12,8},{16,20},{20,16},{24,28},{28,24},{1,5},{5... | collective-permute-start | bytes 442376 | tf_op jit(solution)/shard_map/ppermute | solution.py:411
  5.9 11.3 %collective-permute-start.2 = (bf16[1,144,512]{2,1,0:T(8,128)(2,1)S(1)}, bf16[1,144,512]{2,1,0:T(8,128)(2,1)S(1)}, u32[]{:S(2)}, u32[]{:S(2)}) collective-permute-start(bf16[1,144,512]{2,1,0:T(8,128)(2,1)S(1)} %get-tuple-element.57), channel_id=1, source_target_pairs={{4,8},{12,16},{20,24},{8,4},{16,12},{24,20},{5,9},{13,17},{21,25},... | collective-permute-start | bytes 442376 | tf_op jit(solution)/shard_map/ppermute | solution.py:412
  8.4 15.1 %collective-permute-start.8 = (bf16[2,144,512]{2,1,0:T(8,128)(2,1)S(1)}, bf16[2,144,512]{2,1,0:T(8,128)(2,1)S(1)}, u32[]{:S(2)}, u32[]{:S(2)}) collective-permute-start(bf16[2,144,512]{2,1,0:T(8,128)(2,1)S(1)} %get-tuple-element.33.refs_0_), channel_id=1, source_target_pairs={{0,1},{1,0},{2,3},{3,2},{4,5},{5,4},{6,7},{7,6},{8,9},{9,8},{10,11... | collective-permute-start | bytes 884744 | tf_op jit(solution)/shard_map/ppermute | solution.py:417
  10.0 0.9 copy-start.1
  10.9 0.7 copy-start.2
  11.6 0.7 copy-start.3
  19.2 8.0 %collective-permute-start.3 = (bf16[2,144,512]{2,1,0:T(8,128)(2,1)S(1)}, bf16[2,144,512]{2,1,0:T(8,128)(2,1)S(1)}, u32[]{:S(2)}, u32[]{:S(2)}) collective-permute-start(bf16[2,144,512]{2,1,0:T(8,128)(2,1)S(1)} %get-tuple-element.33.refs_0_), channel_id=1, source_target_pairs={{1,2},{2,1},{5,6},{6,5},{9,10},{10,9},{13,14},{14,13},{17,18},{18,... | collective-permute-start | bytes 884744 | tf_op jit(solution)/shard_map/ppermute | solution.py:418
  19.9 10.3 %collective-permute-start.4 = (bf16[2,144,512]{2,1,0:T(8,128)(2,1)S(1)}, bf16[2,144,512]{2,1,0:T(8,128)(2,1)S(1)}, u32[]{:S(2)}, u32[]{:S(2)}) collective-permute-start(bf16[2,144,512]{2,1,0:T(8,128)(2,1)S(1)} %collective-permute-done.refs_2_), channel_id=1, source_target_pairs={{2,3},{1,0},{6,7},{5,4},{10,11},{9,8},{14,15},{13,12},{18,19},{17,... | collective-permute-start | bytes 884744 | tf_op jit(solution)/shard_map/ppermute | solution.py:419
  23.6 11.3 %collective-permute-start.11 = (bf16[2,144,512]{2,1,0:T(8,128)(2,1)S(1)}, bf16[2,144,512]{2,1,0:T(8,128)(2,1)S(1)}, u32[]{:S(2)}, u32[]{:S(2)}) collective-permute-start(bf16[2,144,512]{2,1,0:T(8,128)(2,1)S(1)} %pad_maximum_fusion.3), channel_id=1, source_target_pairs={{4,8},{12,16},{20,24},{8,4},{16,12},{24,20},{5,9},{13,17},{21,25},... | collective-permute-start | bytes 884744 | tf_op jit(solution)/shard_map/ppermute | solution.py:412
  25.6 9.4 %collective-permute-start.9 = (bf16[2,144,512]{2,1,0:T(8,128)(2,1)S(1)}, bf16[2,144,512]{2,1,0:T(8,128)(2,1)S(1)}, u32[]{:S(2)}, u32[]{:S(2)}) collective-permute-start(bf16[2,144,512]{2,1,0:T(8,128)(2,1)S(1)} %pad_maximum_fusion.2), channel_id=1, source_target_pairs={{0,4},{4,0},{8,12},{12,8},{16,20},{20,16},{24,28},{28,24},{1,5},{5... | collective-permute-start | bytes 884744 | tf_op jit(solution)/shard_map/ppermute | solution.py:411
  30.3 21.7 %collective-permute-start.5 = (bf16[2,112,512]{2,1,0:T(8,128)(2,1)S(1)}, bf16[2,112,512]{2,1,0:T(8,128)(2,1)S(1)}, u32[]{:S(2)}, u32[]{:S(2)}) collective-permute-start(bf16[2,112,512]{2,1,0:T(8,128)(2,1)S(1)} %get-tuple-element.44.refs_0_), channel_id=1, source_target_pairs={{0,1},{1,0},{2,3},{3,2},{4,5},{5,4},{6,7},{7,6},{8,9},{9,8},{10,11... | collective-permute-start | bytes 688136 | tf_op jit(solution)/shard_map/ppermute | solution.py:424
  30.8 21.2 %collective-permute-start.6 = (bf16[2,112,512]{2,1,0:T(8,128)(2,1)S(1)}, bf16[2,112,512]{2,1,0:T(8,128)(2,1)S(1)}, u32[]{:S(2)}, u32[]{:S(2)}) collective-permute-start(bf16[2,112,512]{2,1,0:T(8,128)(2,1)S(1)} %get-tuple-element.44.refs_0_), channel_id=1, source_target_pairs={{0,2},{1,3},{2,0},{3,1},{4,6},{5,7},{6,4},{7,5},{8,10},{9,11},{10,... | collective-permute-start | bytes 688136 | tf_op jit(solution)/shard_map/ppermute | solution.py:424
  34.9 17.2 %collective-permute-start.7 = (bf16[2,112,512]{2,1,0:T(8,128)(2,1)S(1)}, bf16[2,112,512]{2,1,0:T(8,128)(2,1)S(1)}, u32[]{:S(2)}, u32[]{:S(2)}) collective-permute-start(bf16[2,112,512]{2,1,0:T(8,128)(2,1)S(1)} %get-tuple-element.44.refs_0_), channel_id=1, source_target_pairs={{0,3},{1,2},{2,1},{3,0},{4,7},{5,6},{6,5},{7,4},{8,11},{9,10},{10,... | collective-permute-start | bytes 688136 | tf_op jit(solution)/shard_map/ppermute | solution.py:424
  34.9 6.6 %collective-permute-start.10 = (bf16[1,144,512]{2,1,0:T(8,128)(2,1)S(1)}, bf16[1,144,512]{2,1,0:T(8,128)(2,1)S(1)}, u32[]{:S(2)}, u32[]{:S(2)}) collective-permute-start(bf16[1,144,512]{2,1,0:T(8,128)(2,1)S(1)} %get-tuple-element.56), channel_id=1, source_target_pairs={{0,4},{4,0},{8,12},{12,8},{16,20},{20,16},{24,28},{28,24},{1,5},{5... | collective-permute-start | bytes 442376 | tf_op jit(solution)/shard_map/ppermute | solution.py:411
  34.9 6.5 %collective-permute-start.12 = (bf16[1,144,512]{2,1,0:T(8,128)(2,1)S(1)}, bf16[1,144,512]{2,1,0:T(8,128)(2,1)S(1)}, u32[]{:S(2)}, u32[]{:S(2)}) collective-permute-start(bf16[1,144,512]{2,1,0:T(8,128)(2,1)S(1)} %get-tuple-element.55), channel_id=1, source_target_pairs={{4,8},{12,16},{20,24},{8,4},{16,12},{24,20},{5,9},{13,17},{21,25},... | collective-permute-start | bytes 442376 | tf_op jit(solution)/shard_map/ppermute | solution.py:412
  37.5 10.7 %slice-start = ((s8[6307840]{0:T(1024)(128)(4,1)}), s8[4194304]{0:T(1024)(128)(4,1)S(1)}, s32[]{:S(2)}) async-start(s8[6307840]{0:T(1024)(128)(4,1)} %bitcast.1), calls=%async_computation | async-start | bytes 8388608
  41.4 6.8 %slice-start.1 = ((s8[6307840]{0:T(1024)(128)(4,1)}), s8[2113536]{0:T(1024)(128)(4,1)S(1)}, s32[]{:S(2)}) async-start(s8[6307840]{0:T(1024)(128)(4,1)} %bitcast.1), calls=%async_computation.1 | async-start | bytes 4227072
  48.9 8.5 %collective-permute-start.14 = (bf16[1120,128]{1,0:T(8,128)(2,1)S(1)}, bf16[1120,128]{1,0:T(8,128)(2,1)S(1)}, u32[]{:S(2)}, u32[]{:S(2)}) collective-permute-start(bf16[1120,128]{1,0:T(8,128)(2,1)S(1)} %project_3.2), channel_id=1, source_target_pairs={{0,1},{3,2},{4,5},{7,6},{8,9},{11,10},{12,13},{15,14},{16,17},{19,... | collective-permute-start | bytes 860168 | tf_op jit(solution)/shard_map/ppermute | solution.py:503
  51.4 6.0 %collective-permute-start.15 = (bf16[1120,128]{1,0:T(8,128)(2,1)S(1)}, bf16[1120,128]{1,0:T(8,128)(2,1)S(1)}, u32[]{:S(2)}, u32[]{:S(2)}) collective-permute-start(bf16[1120,128]{1,0:T(8,128)(2,1)S(1)} %project_3.2), channel_id=1, source_target_pairs={{1,2},{2,1},{5,6},{6,5},{9,10},{10,9},{13,14},{14,13},{17,18},{18,... | collective-permute-start | bytes 860168 | tf_op jit(solution)/shard_map/ppermute | solution.py:504
  52.2 15.1 %collective-permute-start.13 = (bf16[4,112,512]{2,1,0:T(8,128)(2,1)S(1)}, bf16[4,112,512]{2,1,0:T(8,128)(2,1)S(1)}, u32[]{:S(2)}, u32[]{:S(2)}) collective-permute-start(bf16[4,112,512]{2,1,0:T(8,128)(2,1)S(1)} %pad_maximum_fusion), channel_id=1, source_target_pairs={{0,4},{4,0},{8,12},{12,8},{16,20},{20,16},{24,28},{28,24},{1,5},{5... | collective-permute-start | bytes 1376264 | tf_op jit(solution)/shard_map/ppermute | solution.py:411
  54.6 12.7 %collective-permute-start.16 = (bf16[4,112,512]{2,1,0:T(8,128)(2,1)S(1)}, bf16[4,112,512]{2,1,0:T(8,128)(2,1)S(1)}, u32[]{:S(2)}, u32[]{:S(2)}) collective-permute-start(bf16[4,112,512]{2,1,0:T(8,128)(2,1)S(1)} %pad_maximum_fusion.1), channel_id=1, source_target_pairs={{4,8},{12,16},{20,24},{8,4},{16,12},{24,20},{5,9},{13,17},{21,25},... | collective-permute-start | bytes 1376264 | tf_op jit(solution)/shard_map/ppermute | solution.py:412
  58.1 17.8 %collective-permute-start.18 = (bf16[1120,128]{1,0:T(8,128)(2,1)S(1)}, bf16[1120,128]{1,0:T(8,128)(2,1)S(1)}, u32[]{:S(2)}, u32[]{:S(2)}) collective-permute-start(bf16[1120,128]{1,0:T(8,128)(2,1)S(1)} %project_1.2), channel_id=1, source_target_pairs={{0,1},{1,0},{2,3},{3,2},{4,5},{5,4},{6,7},{7,6},{8,9},{9,8},{10,11... | collective-permute-start | bytes 860168 | tf_op jit(solution)/shard_map/ppermute | solution.py:511
  62.5 13.4 %collective-permute-start.17 = (bf16[1120,128]{1,0:T(8,128)(2,1)S(1)}, bf16[1120,128]{1,0:T(8,128)(2,1)S(1)}, u32[]{:S(2)}, u32[]{:S(2)}) collective-permute-start(bf16[1120,128]{1,0:T(8,128)(2,1)S(1)} %project_2.2), channel_id=1, source_target_pairs={{0,2},{1,3},{2,0},{3,1},{4,6},{5,7},{6,4},{7,5},{8,10},{9,11},{10,... | collective-permute-start | bytes 860168 | tf_op jit(solution)/shard_map/ppermute | solution.py:510
  76.5 15.5 %copy-start.5 = (s32[4]{0:T(128)S(1)}, s32[4]{0:T(128)}, u32[]{:S(2)}) copy-start(s32[4]{0:T(128)} %width_ref.5) | copy-start | bytes 52
  76.5 10.9 %collective-permute-start.19 = (bf16[848,128]{1,0:T(8,128)(2,1)S(1)}, bf16[848,128]{1,0:T(8,128)(2,1)S(1)}, u32[]{:S(2)}, u32[]{:S(2)}) collective-permute-start(bf16[848,128]{1,0:T(8,128)(2,1)S(1)} %project_3.3), channel_id=1, source_target_pairs={{0,1},{3,2},{4,5},{7,6},{8,9},{11,10},{12,13},{15,14},{16,17},{19,... | collective-permute-start | bytes 651272 | tf_op jit(solution)/shard_map/ppermute | solution.py:503
  82.7 4.8 %collective-permute-start.20 = (bf16[848,128]{1,0:T(8,128)(2,1)S(1)}, bf16[848,128]{1,0:T(8,128)(2,1)S(1)}, u32[]{:S(2)}, u32[]{:S(2)}) collective-permute-start(bf16[848,128]{1,0:T(8,128)(2,1)S(1)} %project_3.3), channel_id=1, source_target_pairs={{1,2},{2,1},{5,6},{6,5},{9,10},{10,9},{13,14},{14,13},{17,18},{18,... | collective-permute-start | bytes 651272 | tf_op jit(solution)/shard_map/ppermute | solution.py:504
  88.1 12.1 %collective-permute-start.22 = (bf16[848,128]{1,0:T(8,128)(2,1)S(1)}, bf16[848,128]{1,0:T(8,128)(2,1)S(1)}, u32[]{:S(2)}, u32[]{:S(2)}) collective-permute-start(bf16[848,128]{1,0:T(8,128)(2,1)S(1)} %project_1.3), channel_id=1, source_target_pairs={{0,1},{1,0},{2,3},{3,2},{4,5},{5,4},{6,7},{7,6},{8,9},{9,8},{10,11... | collective-permute-start | bytes 651272 | tf_op jit(solution)/shard_map/ppermute | solution.py:511
  92.0 11.8 %collective-permute-start.21 = (bf16[848,128]{1,0:T(8,128)(2,1)S(1)}, bf16[848,128]{1,0:T(8,128)(2,1)S(1)}, u32[]{:S(2)}, u32[]{:S(2)}) collective-permute-start(bf16[848,128]{1,0:T(8,128)(2,1)S(1)} %project_2.3), channel_id=1, source_target_pairs={{0,2},{1,3},{2,0},{3,1},{4,6},{5,7},{6,4},{7,5},{8,10},{9,11},{10,... | collective-permute-start | bytes 651272 | tf_op jit(solution)/shard_map/ppermute | solution.py:510
where the time goes:
time: 106 us
  starting transfers between devices  44.1 us (42%)
  Pallas kernels  31.7 us (30%)
  waiting for transfers between devices  24.6 us (23%)
  local copies, waits for them, and re-layouts  4.87 us (5%)
    pallas_call x2, Pallas kernels, on_device_packed(): pl.pallas_call(functools.partial(hidden_kernel, chunk=chunk, shards=shard...  11.8 us
    ppermute x2, waiting for transfers between devices, on_device_packed(): lax.ppermute(after(close, relayed), 'tensor', near)  10.3 us
    ppermute x4, starting transfers between devices, send_rows(): lax.ppermute(x, 'row', beyond)  9.08 us
    ppermute x2, starting transfers between devices, on_device_packed(): relayed = lax.ppermute(far, 'tensor', from_end)  8.6 us
    ppermute x2, starting transfers between devices, on_device_packed(): lax.ppermute(after(close, relayed), 'tensor', near)  8.26 us
    pallas_call x2, Pallas kernels, on_device_packed(): pl.pallas_call(functools.partial(own_kernel, chunk=chunk, shards=shards),...  6.96 us
    pallas_call x1, Pallas kernels, on_device_packed(): pl.pallas_call(functools.partial(load_kernel, shards=shards, depth=depth)...  4.76 us
    unnamed x18, local copies, waits for them, and re-layouts  4.72 us
  transfers between devices with their start and end apart: 23, of which 7 were waited for; matrix products, arithmetic and copies ran while one was open for 0% of the time, Pallas kernels for 26%

commit v1 on v0

--- a/solution.py
+++ b/solution.py
@@ -396,6 +396,7 @@
     beyond = beyond + [(b, a) for a, b in beyond]
     near = [(i, i ^ 1) for i in range(4)]
     two_off = [(i, i ^ 2) for i in range(4)]
+    opposite = [(i, i ^ 3) for i in range(4)]
     middle = [(1, 2), (2, 1)]
     to_end = [(2, 3), (1, 0)]
     from_end = [(0, 1), (3, 2)]
@@ -498,18 +499,22 @@
             )(project_turned, hidden, *added)
 
         if number:
-            hidden = after(hidden, *arrived)
-        far = unit(3)
-        relayed = lax.ppermute(far, "tensor", from_end)
-        across = lax.ppermute(far, "tensor", middle)
-        close = unit(1)
-        relayed, across = lax.optimization_barrier((relayed, across))
-        last_unit = unit(2, relayed)
-        arrived = [
-            across,
-            lax.ppermute(last_unit, "tensor", two_off),
-            lax.ppermute(after(close, relayed), "tensor", near),
-        ]
+            units = lax.optimization_barrier((unit(3), unit(2), unit(1), *arrived))[:3]
+            arrived = [
+                lax.ppermute(u, "tensor", pairs) for u, pairs in zip(units, (opposite, two_off, near))
+            ]
+        else:
+            far = unit(3)
+            relayed = lax.ppermute(far, "tensor", from_end)
+            across = lax.ppermute(far, "tensor", middle)
+            close = unit(1)
+            relayed, across = lax.optimization_barrier((relayed, across))
+            last_unit = unit(2, relayed)
+            arrived = [
+                across,
+                lax.ppermute(last_unit, "tensor", two_off),
+                lax.ppermute(after(close, relayed), "tensor", near),
+            ]
         extra = [] if out is None else [out]
         out = pl.pallas_call(
             functools.partial(final_kernel, chunk=chunk, sources=len(arrived)),

time: 106 us -> 103 us (0.972)
  starting transfers between devices: 44.1 us -> 40.3 us
    ppermute x0 -> x3, waiting for transfers between devices: none -> 16.7 us  [on_device_packed(): lax.ppermute(u, 'tensor', pairs)]
    ppermute x2 -> x1, waiting for transfers between devices: 10.3 us -> 1.3 us  [on_device_packed(): lax.ppermute(after(close, relayed), 'tensor', near)]
    ppermute x0 -> x3, starting transfers between devices: none -> 6.9 us  [on_device_packed(): lax.ppermute(u, 'tensor', pairs)]
    ppermute x2 -> x1, starting transfers between devices: 8.6 us -> 2.48 us  [on_device_packed(): relayed = lax.ppermute(far, 'tensor', from_end)]
    ppermute x2 -> x1, starting transfers between devices: 8.26 us -> 4.42 us  [on_device_packed(): lax.ppermute(after(close, relayed), 'tensor', near)]
    ppermute x2 -> x1, waiting for transfers between devices: 3.48 us -> 0.01 us  [on_device_packed(): lax.ppermute(last_unit, 'tensor', two_off)]
    ppermute x2 -> x1, waiting for transfers between devices: 3.41 us -> 0.01 us  [on_device_packed(): relayed = lax.ppermute(far, 'tensor', from_end)]
  transfers between devices with their start and end apart: 23 -> 22, of which waited for: 7 -> 6; matrix products, arithmetic and copies ran while one was open for 0% -> 0% of each run, Pallas kernels for 26% -> 28%
where the time goes in v1:
time: 103 us
  starting transfers between devices  40.3 us (39%)
  Pallas kernels  31.7 us (31%)
  waiting for transfers between devices  25.4 us (25%)
  local copies, waits for them, and re-layouts  4.87 us (5%)
    ppermute x3, waiting for transfers between devices, on_device_packed(): lax.ppermute(u, 'tensor', pairs)  16.7 us
    pallas_call x2, Pallas kernels, on_device_packed(): pl.pallas_call(functools.partial(hidden_kernel, chunk=chunk, shards=shard...  11.8 us
    ppermute x4, starting transfers between devices, send_rows(): lax.ppermute(x, 'row', beyond)  9.08 us
    pallas_call x2, Pallas kernels, on_device_packed(): pl.pallas_call(functools.partial(own_kernel, chunk=chunk, shards=shards),...  6.96 us
    ppermute x3, starting transfers between devices, on_device_packed(): lax.ppermute(u, 'tensor', pairs)  6.9 us
    pallas_call x1, Pallas kernels, on_device_packed(): pl.pallas_call(functools.partial(load_kernel, shards=shards, depth=depth)...  4.76 us
    unnamed x18, local copies, waits for them, and re-layouts  4.72 us
    ppermute x3, starting transfers between devices, direct(): lax.ppermute(mine, 'tensor', [(i, i ^ j) for i in range(4)])  4.57 us
  transfers between devices with their start and end apart: 22, of which 6 were waited for; matrix products, arithmetic and copies ran while one was open for 0% of the time, Pallas kernels for 28%

profile of v1, /device:TPU:2, one launch (start us, length us, event | category | flops | bytes accessed | tf_op | source)
XLA Modules:
  0.0 102.9 jit_solution(8243011952319122113)
XLA Ops:
  0.0 1.1 %copy-done = bf16[4,2,64,560]{3,2,1,0:T(8,128)(2,1)S(1)} copy-done((bf16[4,2,64,560]{3,2,1,0:T(8,128)(2,1)S(1)}, bf16[4,2,64,560]{3,2,1,0:T(8,128)(2,1)}, u32[]{:S(2)}) %copy-start) | copy-done | bytes 573464
  1.1 0.7 copy-done.4
  1.7 0.7 copy-done.6
  2.4 0.7 pack.1
  3.1 2.7 %collective-permute-start = (bf16[2,144,512]{2,1,0:T(8,128)(2,1)S(1)}, bf16[2,144,512]{2,1,0:T(8,128)(2,1)S(1)}, u32[]{:S(2)}, u32[]{:S(2)}) collective-permute-start(bf16[2,144,512]{2,1,0:T(8,128)(2,1)S(1)} %get-tuple-element.32.refs_0_), channel_id=1, source_target_pairs={{0,2},{1,3},{2,0},{3,1},{4,6},{5,7},{6,4},{7,5},{8,10},{9,11},{10,... | collective-permute-start | bytes 884744 | tf_op jit(solution)/shard_map/ppermute | solution.py:417
  5.8 0.1 collective-permute-start.1
  5.9 2.5 %collective-permute-start.2 = (bf16[1,144,512]{2,1,0:T(8,128)(2,1)S(1)}, bf16[1,144,512]{2,1,0:T(8,128)(2,1)S(1)}, u32[]{:S(2)}, u32[]{:S(2)}) collective-permute-start(bf16[1,144,512]{2,1,0:T(8,128)(2,1)S(1)} %get-tuple-element.55), channel_id=1, source_target_pairs={{4,8},{12,16},{20,24},{8,4},{16,12},{24,20},{5,9},{13,17},{21,25},... | collective-permute-start | bytes 442376 | tf_op jit(solution)/shard_map/ppermute | solution.py:413
  8.4 1.6 %collective-permute-start.8 = (bf16[2,144,512]{2,1,0:T(8,128)(2,1)S(1)}, bf16[2,144,512]{2,1,0:T(8,128)(2,1)S(1)}, u32[]{:S(2)}, u32[]{:S(2)}) collective-permute-start(bf16[2,144,512]{2,1,0:T(8,128)(2,1)S(1)} %get-tuple-element.32.refs_0_), channel_id=1, source_target_pairs={{0,1},{1,0},{2,3},{3,2},{4,5},{5,4},{6,7},{7,6},{8,9},{9,8},{10,11... | collective-permute-start | bytes 884744 | tf_op jit(solution)/shard_map/ppermute | solution.py:418
  10.0 0.9 copy-done.1
  10.9 0.7 copy-done.2
  11.6 0.7 copy-done.3
  12.3 4.8 %load_weights.1 = (bf16[2,2240,1400]{2,1,0:T(8,128)(2,1)S(1)}, f32[22,1400]{1,0:T(8,128)S(1)}) custom-call(f32[3,3,2,1400]{3,2,1,0:T(2,128)S(1)} %copy-done.1, f32[2,1400]{1,0:T(2,128)S(1)} %copy-done.2, f32[2,1400]{1,0:T(2,128)S(1)} %copy-done.3, bf16[2,2240,1400]{2,1,0:T(8,128)(2,1)} %w_ref), custom_call_target="tpu_custom_call" | custom-call | tf_op jit(solution)/shard_map/load_weights/pallas_call | solution.py:429
  17.1 2.1 %collective-permute-done.refs_2_ = bf16[2,144,512]{2,1,0:T(8,128)(2,1)S(1)} collective-permute-done((bf16[2,144,512]{2,1,0:T(8,128)(2,1)S(1)}, bf16[2,144,512]{2,1,0:T(8,128)(2,1)S(1)}, u32[]{:S(2)}, u32[]{:S(2)}) %collective-permute-start) | collective-permute-done | bytes 294944 | tf_op jit(solution)/shard_map/ppermute | solution.py:417
  19.2 0.7 collective-permute-start.3
  19.9 1.3 %collective-permute-start.4 = (bf16[2,144,512]{2,1,0:T(8,128)(2,1)S(1)}, bf16[2,144,512]{2,1,0:T(8,128)(2,1)S(1)}, u32[]{:S(2)}, u32[]{:S(2)}) collective-permute-start(bf16[2,144,512]{2,1,0:T(8,128)(2,1)S(1)} %collective-permute-done.refs_2_), channel_id=1, source_target_pairs={{2,3},{1,0},{6,7},{5,4},{10,11},{9,8},{14,15},{13,12},{18,19},{17,... | collective-permute-start | bytes 884744 | tf_op jit(solution)/shard_map/ppermute | solution.py:420
  21.2 2.3 %collective-permute-done.8.refs_1_ = bf16[2,144,512]{2,1,0:T(8,128)(2,1)S(1)} collective-permute-done((bf16[2,144,512]{2,1,0:T(8,128)(2,1)S(1)}, bf16[2,144,512]{2,1,0:T(8,128)(2,1)S(1)}, u32[]{:S(2)}, u32[]{:S(2)}) %collective-permute-start.8) | collective-permute-done | bytes 294944 | tf_op jit(solution)/shard_map/ppermute | solution.py:418
  23.6 1.9 %collective-permute-start.11 = (bf16[2,144,512]{2,1,0:T(8,128)(2,1)S(1)}, bf16[2,144,512]{2,1,0:T(8,128)(2,1)S(1)}, u32[]{:S(2)}, u32[]{:S(2)}) collective-permute-start(bf16[2,144,512]{2,1,0:T(8,128)(2,1)S(1)} %pad_maximum_fusion.3), channel_id=1, source_target_pairs={{4,8},{12,16},{20,24},{8,4},{16,12},{24,20},{5,9},{13,17},{21,25},... | collective-permute-start | bytes 884744 | tf_op jit(solution)/shard_map/ppermute | solution.py:413
  25.6 1.7 %collective-permute-start.9 = (bf16[2,144,512]{2,1,0:T(8,128)(2,1)S(1)}, bf16[2,144,512]{2,1,0:T(8,128)(2,1)S(1)}, u32[]{:S(2)}, u32[]{:S(2)}) collective-permute-start(bf16[2,144,512]{2,1,0:T(8,128)(2,1)S(1)} %pad_maximum_fusion.2), channel_id=1, source_target_pairs={{0,4},{4,0},{8,12},{12,8},{16,20},{20,16},{24,28},{28,24},{1,5},{5... | collective-permute-start | bytes 884744 | tf_op jit(solution)/shard_map/ppermute | solution.py:412
  27.3 3.0 %collective-permute-done.4 = bf16[2,144,512]{2,1,0:T(8,128)(2,1)S(1)} collective-permute-done((bf16[2,144,512]{2,1,0:T(8,128)(2,1)S(1)}, bf16[2,144,512]{2,1,0:T(8,128)(2,1)S(1)}, u32[]{:S(2)}, u32[]{:S(2)}) %collective-permute-start.4) | collective-permute-done | bytes 294944 | tf_op jit(solution)/shard_map/ppermute | solution.py:420
  30.2 0.1 add.3.refs_3_
  30.3 0.5 collective-permute-start.5
  30.8 4.1 %collective-permute-start.6 = (bf16[2,112,512]{2,1,0:T(8,128)(2,1)S(1)}, bf16[2,112,512]{2,1,0:T(8,128)(2,1)S(1)}, u32[]{:S(2)}, u32[]{:S(2)}) collective-permute-start(bf16[2,112,512]{2,1,0:T(8,128)(2,1)S(1)} %get-tuple-element.43.refs_0_), channel_id=1, source_target_pairs={{0,2},{1,3},{2,0},{3,1},{4,6},{5,7},{6,4},{7,5},{8,10},{9,11},{10,... | collective-permute-start | bytes 688136 | tf_op jit(solution)/shard_map/ppermute | solution.py:425
  34.9 2.5 %collective-permute-start.12 = (bf16[1,144,512]{2,1,0:T(8,128)(2,1)S(1)}, bf16[1,144,512]{2,1,0:T(8,128)(2,1)S(1)}, u32[]{:S(2)}, u32[]{:S(2)}) collective-permute-start(bf16[1,144,512]{2,1,0:T(8,128)(2,1)S(1)} %get-tuple-element.53), channel_id=1, source_target_pairs={{4,8},{12,16},{20,24},{8,4},{16,12},{24,20},{5,9},{13,17},{21,25},... | collective-permute-start | bytes 442376 | tf_op jit(solution)/shard_map/ppermute | solution.py:413
  37.5 4.0 %expand_own.2.refs_6_ = f32[2,256,1400]{2,1,0:T(8,128)S(1)} custom-call(bf16[2,144,512]{2,1,0:T(8,128)(2,1)S(1)} %get-tuple-element.32.refs_0_, bf16[2,144,512]{2,1,0:T(8,128)(2,1)S(1)} %collective-permute-done.8.refs_1_, bf16[2,144,512]{2,1,0:T(8,128)(2,1)S(1)} %collective-permute-done.refs_2_, bf16[2,144,512]{2,1,0:T(8,128)(2,1)S(1)} %add.3.refs_3_, ...), custom_call_target="tpu_custom_call" | custom-call | flops 1000 | bytes 1000 | tf_op jit(solution)/shard_map/expand_own/pallas_call | solution.py:453
  41.5 6.7 %expand_conv.2.hidden_ref = bf16[256,1400]{1,0:T(8,128)(2,1)S(1)} custom-call(bf16[1,144,512]{2,1,0:T(8,128)(2,1)S(1)} %collective-permute-done.1.refs_0_, bf16[2,144,512]{2,1,0:T(8,128)(2,1)S(1)} %collective-permute-done.9.refs_1_, bf16[1,144,512]{2,1,0:T(8,128)(2,1)S(1)} %collective-permute-done.10.refs_2_, ...), custom_call_target="tpu_custom_call" | custom-call | flops 1000 | bytes 1000 | tf_op jit(solution)/shard_map/expand_conv/pallas_call | solution.py:469
  48.2 0.6 project_3.2
  48.9 2.5 %collective-permute-start.14 = (bf16[1120,128]{1,0:T(8,128)(2,1)S(1)}, bf16[1120,128]{1,0:T(8,128)(2,1)S(1)}, u32[]{:S(2)}, u32[]{:S(2)}) collective-permute-start(bf16[1120,128]{1,0:T(8,128)(2,1)S(1)} %project_3.2), channel_id=1, source_target_pairs={{0,1},{3,2},{4,5},{7,6},{8,9},{11,10},{12,13},{15,14},{16,17},{19,... | collective-permute-start | bytes 860168 | tf_op jit(solution)/shard_map/ppermute | solution.py:508
  51.4 0.7 collective-permute-start.15
  52.2 0.1 pad_maximum_fusion
  52.2 2.3 %collective-permute-start.13 = (bf16[4,112,512]{2,1,0:T(8,128)(2,1)S(1)}, bf16[4,112,512]{2,1,0:T(8,128)(2,1)S(1)}, u32[]{:S(2)}, u32[]{:S(2)}) collective-permute-start(bf16[4,112,512]{2,1,0:T(8,128)(2,1)S(1)} %pad_maximum_fusion), channel_id=1, source_target_pairs={{0,4},{4,0},{8,12},{12,8},{16,20},{20,16},{24,28},{28,24},{1,5},{5... | collective-permute-start | bytes 1376264 | tf_op jit(solution)/shard_map/ppermute | solution.py:412
  54.6 0.1 pad_maximum_fusion.1
  54.6 2.1 %collective-permute-start.16 = (bf16[4,112,512]{2,1,0:T(8,128)(2,1)S(1)}, bf16[4,112,512]{2,1,0:T(8,128)(2,1)S(1)}, u32[]{:S(2)}, u32[]{:S(2)}) collective-permute-start(bf16[4,112,512]{2,1,0:T(8,128)(2,1)S(1)} %pad_maximum_fusion.1), channel_id=1, source_target_pairs={{4,8},{12,16},{20,24},{8,4},{16,12},{24,20},{5,9},{13,17},{21,25},... | collective-permute-start | bytes 1376264 | tf_op jit(solution)/shard_map/ppermute | solution.py:413
  56.7 0.6 project_1.3
  57.4 0.6 project_2.2
  58.1 4.4 %collective-permute-start.18 = (bf16[1120,128]{1,0:T(8,128)(2,1)S(1)}, bf16[1120,128]{1,0:T(8,128)(2,1)S(1)}, u32[]{:S(2)}, u32[]{:S(2)}) collective-permute-start(bf16[1120,128]{1,0:T(8,128)(2,1)S(1)} %project_1.3), channel_id=1, source_target_pairs={{0,1},{1,0},{2,3},{3,2},{4,5},{5,4},{6,7},{7,6},{8,9},{9,8},{10,11... | collective-permute-start | bytes 860168 | tf_op jit(solution)/shard_map/ppermute | solution.py:516
  62.5 1.8 %collective-permute-start.17 = (bf16[1120,128]{1,0:T(8,128)(2,1)S(1)}, bf16[1120,128]{1,0:T(8,128)(2,1)S(1)}, u32[]{:S(2)}, u32[]{:S(2)}) collective-permute-start(bf16[1120,128]{1,0:T(8,128)(2,1)S(1)} %project_2.2), channel_id=1, source_target_pairs={{0,2},{1,3},{2,0},{3,1},{4,6},{5,7},{6,4},{7,5},{8,10},{9,11},{10,... | collective-permute-start | bytes 860168 | tf_op jit(solution)/shard_map/ppermute | solution.py:515
  64.3 3.0 %expand_own.3.refs_2_ = f32[2,192,1400]{2,1,0:T(8,128)S(1)} custom-call(bf16[2,112,512]{2,1,0:T(8,128)(2,1)S(1)} %get-tuple-element.43.refs_0_, bf16[2,112,512]{2,1,0:T(8,128)(2,1)S(1)} %collective-permute-done.5.refs_1_, bf16[2,112,512]{2,1,0:T(8,128)(2,1)S(1)} %collective-permute-done.6.refs_2_, bf16[2,112,512]{2,1,0:T(8,128)(2,1)S(1)} %collective-permute-done.7.refs_3_, ...), custom_call_target="tpu_custom_call" | custom-call | flops 1000 | bytes 1000 | tf_op jit(solution)/shard_map/expand_own/pallas_call | solution.py:453
  67.3 5.1 %expand_conv.3.hidden_ref = bf16[192,1400]{1,0:T(8,128)(2,1)S(1)} custom-call(bf16[4,112,512]{2,1,0:T(8,128)(2,1)S(1)} %collective-permute-done.13.refs_0_, bf16[4,112,512]{2,1,0:T(8,128)(2,1)S(1)} %collective-permute-done.16.refs_1_, f32[2,192,1400]{2,1,0:T(8,128)S(1)} %expand_own.3.refs_2_, f32[4,96,128]{2,1,0:T(8,128)S(1)} %get-tuple-element.27.refs_4_.refs_3_.mask_ref, ...), custom_call_target="tpu_custom_call" | custom-call | flops 1000 | bytes 1000 | tf_op jit(solution)/shard_map/expand_conv/pallas_call | solution.py:469
  72.4 0.7 project_3.3
  73.1 0.7 project_2.3
  73.8 0.7 project_1.2
  74.5 1.3 %collective-permute-done.18.refs_2_ = bf16[1120,128]{1,0:T(8,128)(2,1)S(1)} collective-permute-done((bf16[1120,128]{1,0:T(8,128)(2,1)S(1)}, bf16[1120,128]{1,0:T(8,128)(2,1)S(1)}, u32[]{:S(2)}, u32[]{:S(2)}) %collective-permute-start.18) | collective-permute-done | bytes 286752 | tf_op jit(solution)/shard_map/ppermute | solution.py:516
  75.8 6.3 %collective-permute-start.19 = (bf16[848,128]{1,0:T(8,128)(2,1)S(1)}, bf16[848,128]{1,0:T(8,128)(2,1)S(1)}, u32[]{:S(2)}, u32[]{:S(2)}) collective-permute-start(bf16[848,128]{1,0:T(8,128)(2,1)S(1)} %project_3.3), channel_id=1, source_target_pairs={{0,3},{1,2},{2,1},{3,0},{4,7},{5,6},{6,5},{7,4},{8,11},{9,10},{10,... | collective-permute-start | bytes 651272 | tf_op jit(solution)/shard_map/ppermute | solution.py:504
  82.2 0.6 collective-permute-start.21
  82.7 1.3 %finish.2.refs_3_ = bf16[4,2,64,560]{3,2,1,0:T(8,128)(2,1)S(1)} custom-call(s32[4]{0:T(128)S(1)} %copy-done.5, f32[4,128,128]{2,1,0:T(8,128)S(1)} %get-tuple-element.35.refs_4_.refs_7_.mask_ref, bf16[2240,1400]{1,0:T(8,128)(2,1)S(1)} %bitcast.9, bf16[256,1400]{1,0:T(8,128)(2,1)S(1)} %expand_conv.2.hidden_ref, ...), custom_call_target="tpu_custom_call" | custom-call | flops 401408000 | bytes 2284800 | tf_op jit(solution)/shard_map/finish/pallas_call | solution.py:519
  84.1 4.4 %collective-permute-done.19.refs_0_ = bf16[848,128]{1,0:T(8,128)(2,1)S(1)} collective-permute-done((bf16[848,128]{1,0:T(8,128)(2,1)S(1)}, bf16[848,128]{1,0:T(8,128)(2,1)S(1)}, u32[]{:S(2)}, u32[]{:S(2)}) %collective-permute-start.19) | collective-permute-done | bytes 217120 | tf_op jit(solution)/shard_map/ppermute | solution.py:504
  88.5 12.2 %collective-permute-done.20.refs_1_ = bf16[848,128]{1,0:T(8,128)(2,1)S(1)} collective-permute-done((bf16[848,128]{1,0:T(8,128)(2,1)S(1)}, bf16[848,128]{1,0:T(8,128)(2,1)S(1)}, u32[]{:S(2)}, u32[]{:S(2)}) %collective-permute-start.20) | collective-permute-done | bytes 217120 | tf_op jit(solution)/shard_map/ppermute | solution.py:504
  100.7 2.2 %finish.3 = bf16[4,2,64,560]{3,2,1,0:T(8,128)(2,1)} custom-call(s32[4]{0:T(128)S(1)} %copy-done.5, f32[4,96,128]{2,1,0:T(8,128)S(1)} %get-tuple-element.27.refs_4_.refs_3_.mask_ref, bf16[2240,1400]{1,0:T(8,128)(2,1)S(1)} %bitcast.10, bf16[192,1400]{1,0:T(8,128)(2,1)S(1)} %expand_conv.3.hidden_ref, bf16[848,128]{1,0:T(8,128)(2,1)S(1)} %collective-permute-done.19.refs_0_, ...), custom_call_target="tpu_custom_call" | custom-call | flops 301056000 | bytes 2105600 | tf_op jit(solution)/shard_map/finish/pallas_call | solution.py:519
  (40 shorter events, 0.3 us)
Async XLA Ops:
  0.0 1.1 %copy-start = (bf16[4,2,64,560]{3,2,1,0:T(8,128)(2,1)S(1)}, bf16[4,2,64,560]{3,2,1,0:T(8,128)(2,1)}, u32[]{:S(2)}) copy-start(bf16[4,2,64,560]{3,2,1,0:T(8,128)(2,1)} %x_ref.1) | copy-start | bytes 1720324
  1.1 0.7 copy-start.4
  1.7 0.7 copy-start.6
  3.1 16.1 %collective-permute-start = (bf16[2,144,512]{2,1,0:T(8,128)(2,1)S(1)}, bf16[2,144,512]{2,1,0:T(8,128)(2,1)S(1)}, u32[]{:S(2)}, u32[]{:S(2)}) collective-permute-start(bf16[2,144,512]{2,1,0:T(8,128)(2,1)S(1)} %get-tuple-element.32.refs_0_), channel_id=1, source_target_pairs={{0,2},{1,3},{2,0},{3,1},{4,6},{5,7},{6,4},{7,5},{8,10},{9,11},{10,... | collective-permute-start | bytes 884744 | tf_op jit(solution)/shard_map/ppermute | solution.py:417
  5.8 11.3 %collective-permute-start.1 = (bf16[1,144,512]{2,1,0:T(8,128)(2,1)S(1)}, bf16[1,144,512]{2,1,0:T(8,128)(2,1)S(1)}, u32[]{:S(2)}, u32[]{:S(2)}) collective-permute-start(bf16[1,144,512]{2,1,0:T(8,128)(2,1)S(1)} %get-tuple-element.56), channel_id=1, source_target_pairs={{0,4},{4,0},{8,12},{12,8},{16,20},{20,16},{24,28},{28,24},{1,5},{5... | collective-permute-start | bytes 442376 | tf_op jit(solution)/shard_map/ppermute | solution.py:412
  5.9 11.3 %collective-permute-start.2 = (bf16[1,144,512]{2,1,0:T(8,128)(2,1)S(1)}, bf16[1,144,512]{2,1,0:T(8,128)(2,1)S(1)}, u32[]{:S(2)}, u32[]{:S(2)}) collective-permute-start(bf16[1,144,512]{2,1,0:T(8,128)(2,1)S(1)} %get-tuple-element.55), channel_id=1, source_target_pairs={{4,8},{12,16},{20,24},{8,4},{16,12},{24,20},{5,9},{13,17},{21,25},... | collective-permute-start | bytes 442376 | tf_op jit(solution)/shard_map/ppermute | solution.py:413
  8.4 15.1 %collective-permute-start.8 = (bf16[2,144,512]{2,1,0:T(8,128)(2,1)S(1)}, bf16[2,144,512]{2,1,0:T(8,128)(2,1)S(1)}, u32[]{:S(2)}, u32[]{:S(2)}) collective-permute-start(bf16[2,144,512]{2,1,0:T(8,128)(2,1)S(1)} %get-tuple-element.32.refs_0_), channel_id=1, source_target_pairs={{0,1},{1,0},{2,3},{3,2},{4,5},{5,4},{6,7},{7,6},{8,9},{9,8},{10,11... | collective-permute-start | bytes 884744 | tf_op jit(solution)/shard_map/ppermute | solution.py:418
  10.0 0.9 copy-start.1
  10.9 0.7 copy-start.2
  11.6 0.7 copy-start.3
  19.2 8.0 %collective-permute-start.3 = (bf16[2,144,512]{2,1,0:T(8,128)(2,1)S(1)}, bf16[2,144,512]{2,1,0:T(8,128)(2,1)S(1)}, u32[]{:S(2)}, u32[]{:S(2)}) collective-permute-start(bf16[2,144,512]{2,1,0:T(8,128)(2,1)S(1)} %get-tuple-element.32.refs_0_), channel_id=1, source_target_pairs={{1,2},{2,1},{5,6},{6,5},{9,10},{10,9},{13,14},{14,13},{17,18},{18,... | collective-permute-start | bytes 884744 | tf_op jit(solution)/shard_map/ppermute | solution.py:419
  19.9 10.3 %collective-permute-start.4 = (bf16[2,144,512]{2,1,0:T(8,128)(2,1)S(1)}, bf16[2,144,512]{2,1,0:T(8,128)(2,1)S(1)}, u32[]{:S(2)}, u32[]{:S(2)}) collective-permute-start(bf16[2,144,512]{2,1,0:T(8,128)(2,1)S(1)} %collective-permute-done.refs_2_), channel_id=1, source_target_pairs={{2,3},{1,0},{6,7},{5,4},{10,11},{9,8},{14,15},{13,12},{18,19},{17,... | collective-permute-start | bytes 884744 | tf_op jit(solution)/shard_map/ppermute | solution.py:420
  23.6 11.3 %collective-permute-start.11 = (bf16[2,144,512]{2,1,0:T(8,128)(2,1)S(1)}, bf16[2,144,512]{2,1,0:T(8,128)(2,1)S(1)}, u32[]{:S(2)}, u32[]{:S(2)}) collective-permute-start(bf16[2,144,512]{2,1,0:T(8,128)(2,1)S(1)} %pad_maximum_fusion.3), channel_id=1, source_target_pairs={{4,8},{12,16},{20,24},{8,4},{16,12},{24,20},{5,9},{13,17},{21,25},... | collective-permute-start | bytes 884744 | tf_op jit(solution)/shard_map/ppermute | solution.py:413
  25.6 9.4 %collective-permute-start.9 = (bf16[2,144,512]{2,1,0:T(8,128)(2,1)S(1)}, bf16[2,144,512]{2,1,0:T(8,128)(2,1)S(1)}, u32[]{:S(2)}, u32[]{:S(2)}) collective-permute-start(bf16[2,144,512]{2,1,0:T(8,128)(2,1)S(1)} %pad_maximum_fusion.2), channel_id=1, source_target_pairs={{0,4},{4,0},{8,12},{12,8},{16,20},{20,16},{24,28},{28,24},{1,5},{5... | collective-permute-start | bytes 884744 | tf_op jit(solution)/shard_map/ppermute | solution.py:412
  30.3 21.7 %collective-permute-start.5 = (bf16[2,112,512]{2,1,0:T(8,128)(2,1)S(1)}, bf16[2,112,512]{2,1,0:T(8,128)(2,1)S(1)}, u32[]{:S(2)}, u32[]{:S(2)}) collective-permute-start(bf16[2,112,512]{2,1,0:T(8,128)(2,1)S(1)} %get-tuple-element.43.refs_0_), channel_id=1, source_target_pairs={{0,1},{1,0},{2,3},{3,2},{4,5},{5,4},{6,7},{7,6},{8,9},{9,8},{10,11... | collective-permute-start | bytes 688136 | tf_op jit(solution)/shard_map/ppermute | solution.py:425
  30.8 21.2 %collective-permute-start.6 = (bf16[2,112,512]{2,1,0:T(8,128)(2,1)S(1)}, bf16[2,112,512]{2,1,0:T(8,128)(2,1)S(1)}, u32[]{:S(2)}, u32[]{:S(2)}) collective-permute-start(bf16[2,112,512]{2,1,0:T(8,128)(2,1)S(1)} %get-tuple-element.43.refs_0_), channel_id=1, source_target_pairs={{0,2},{1,3},{2,0},{3,1},{4,6},{5,7},{6,4},{7,5},{8,10},{9,11},{10,... | collective-permute-start | bytes 688136 | tf_op jit(solution)/shard_map/ppermute | solution.py:425
  34.9 17.2 %collective-permute-start.7 = (bf16[2,112,512]{2,1,0:T(8,128)(2,1)S(1)}, bf16[2,112,512]{2,1,0:T(8,128)(2,1)S(1)}, u32[]{:S(2)}, u32[]{:S(2)}) collective-permute-start(bf16[2,112,512]{2,1,0:T(8,128)(2,1)S(1)} %get-tuple-element.43.refs_0_), channel_id=1, source_target_pairs={{0,3},{1,2},{2,1},{3,0},{4,7},{5,6},{6,5},{7,4},{8,11},{9,10},{10,... | collective-permute-start | bytes 688136 | tf_op jit(solution)/shard_map/ppermute | solution.py:425
  34.9 6.6 %collective-permute-start.10 = (bf16[1,144,512]{2,1,0:T(8,128)(2,1)S(1)}, bf16[1,144,512]{2,1,0:T(8,128)(2,1)S(1)}, u32[]{:S(2)}, u32[]{:S(2)}) collective-permute-start(bf16[1,144,512]{2,1,0:T(8,128)(2,1)S(1)} %get-tuple-element.54), channel_id=1, source_target_pairs={{0,4},{4,0},{8,12},{12,8},{16,20},{20,16},{24,28},{28,24},{1,5},{5... | collective-permute-start | bytes 442376 | tf_op jit(solution)/shard_map/ppermute | solution.py:412
  34.9 6.5 %collective-permute-start.12 = (bf16[1,144,512]{2,1,0:T(8,128)(2,1)S(1)}, bf16[1,144,512]{2,1,0:T(8,128)(2,1)S(1)}, u32[]{:S(2)}, u32[]{:S(2)}) collective-permute-start(bf16[1,144,512]{2,1,0:T(8,128)(2,1)S(1)} %get-tuple-element.53), channel_id=1, source_target_pairs={{4,8},{12,16},{20,24},{8,4},{16,12},{24,20},{5,9},{13,17},{21,25},... | collective-permute-start | bytes 442376 | tf_op jit(solution)/shard_map/ppermute | solution.py:413
  37.5 10.7 %slice-start = ((s8[6307840]{0:T(1024)(128)(4,1)}), s8[4194304]{0:T(1024)(128)(4,1)S(1)}, s32[]{:S(2)}) async-start(s8[6307840]{0:T(1024)(128)(4,1)} %bitcast.1), calls=%async_computation | async-start | bytes 8388608
  41.4 6.8 %slice-start.1 = ((s8[6307840]{0:T(1024)(128)(4,1)}), s8[2113536]{0:T(1024)(128)(4,1)S(1)}, s32[]{:S(2)}) async-start(s8[6307840]{0:T(1024)(128)(4,1)} %bitcast.1), calls=%async_computation.1 | async-start | bytes 4227072
  48.9 8.5 %collective-permute-start.14 = (bf16[1120,128]{1,0:T(8,128)(2,1)S(1)}, bf16[1120,128]{1,0:T(8,128)(2,1)S(1)}, u32[]{:S(2)}, u32[]{:S(2)}) collective-permute-start(bf16[1120,128]{1,0:T(8,128)(2,1)S(1)} %project_3.2), channel_id=1, source_target_pairs={{0,1},{3,2},{4,5},{7,6},{8,9},{11,10},{12,13},{15,14},{16,17},{19,... | collective-permute-start | bytes 860168 | tf_op jit(solution)/shard_map/ppermute | solution.py:508
  51.4 6.0 %collective-permute-start.15 = (bf16[1120,128]{1,0:T(8,128)(2,1)S(1)}, bf16[1120,128]{1,0:T(8,128)(2,1)S(1)}, u32[]{:S(2)}, u32[]{:S(2)}) collective-permute-start(bf16[1120,128]{1,0:T(8,128)(2,1)S(1)} %project_3.2), channel_id=1, source_target_pairs={{1,2},{2,1},{5,6},{6,5},{9,10},{10,9},{13,14},{14,13},{17,18},{18,... | collective-permute-start | bytes 860168 | tf_op jit(solution)/shard_map/ppermute | solution.py:509
  52.2 15.1 %collective-permute-start.13 = (bf16[4,112,512]{2,1,0:T(8,128)(2,1)S(1)}, bf16[4,112,512]{2,1,0:T(8,128)(2,1)S(1)}, u32[]{:S(2)}, u32[]{:S(2)}) collective-permute-start(bf16[4,112,512]{2,1,0:T(8,128)(2,1)S(1)} %pad_maximum_fusion), channel_id=1, source_target_pairs={{0,4},{4,0},{8,12},{12,8},{16,20},{20,16},{24,28},{28,24},{1,5},{5... | collective-permute-start | bytes 1376264 | tf_op jit(solution)/shard_map/ppermute | solution.py:412
  54.6 12.7 %collective-permute-start.16 = (bf16[4,112,512]{2,1,0:T(8,128)(2,1)S(1)}, bf16[4,112,512]{2,1,0:T(8,128)(2,1)S(1)}, u32[]{:S(2)}, u32[]{:S(2)}) collective-permute-start(bf16[4,112,512]{2,1,0:T(8,128)(2,1)S(1)} %pad_maximum_fusion.1), channel_id=1, source_target_pairs={{4,8},{12,16},{20,24},{8,4},{16,12},{24,20},{5,9},{13,17},{21,25},... | collective-permute-start | bytes 1376264 | tf_op jit(solution)/shard_map/ppermute | solution.py:413
  58.1 17.8 %collective-permute-start.18 = (bf16[1120,128]{1,0:T(8,128)(2,1)S(1)}, bf16[1120,128]{1,0:T(8,128)(2,1)S(1)}, u32[]{:S(2)}, u32[]{:S(2)}) collective-permute-start(bf16[1120,128]{1,0:T(8,128)(2,1)S(1)} %project_1.3), channel_id=1, source_target_pairs={{0,1},{1,0},{2,3},{3,2},{4,5},{5,4},{6,7},{7,6},{8,9},{9,8},{10,11... | collective-permute-start | bytes 860168 | tf_op jit(solution)/shard_map/ppermute | solution.py:516
  62.5 13.4 %collective-permute-start.17 = (bf16[1120,128]{1,0:T(8,128)(2,1)S(1)}, bf16[1120,128]{1,0:T(8,128)(2,1)S(1)}, u32[]{:S(2)}, u32[]{:S(2)}) collective-permute-start(bf16[1120,128]{1,0:T(8,128)(2,1)S(1)} %project_2.2), channel_id=1, source_target_pairs={{0,2},{1,3},{2,0},{3,1},{4,6},{5,7},{6,4},{7,5},{8,10},{9,11},{10,... | collective-permute-start | bytes 860168 | tf_op jit(solution)/shard_map/ppermute | solution.py:515
  73.1 9.6 %copy-start.5 = (s32[4]{0:T(128)S(1)}, s32[4]{0:T(128)}, u32[]{:S(2)}) copy-start(s32[4]{0:T(128)} %width_ref.5) | copy-start | bytes 52
  75.8 12.7 %collective-permute-start.19 = (bf16[848,128]{1,0:T(8,128)(2,1)S(1)}, bf16[848,128]{1,0:T(8,128)(2,1)S(1)}, u32[]{:S(2)}, u32[]{:S(2)}) collective-permute-start(bf16[848,128]{1,0:T(8,128)(2,1)S(1)} %project_3.3), channel_id=1, source_target_pairs={{0,3},{1,2},{2,1},{3,0},{4,7},{5,6},{6,5},{7,4},{8,11},{9,10},{10,... | collective-permute-start | bytes 651272 | tf_op jit(solution)/shard_map/ppermute | solution.py:504
  82.2 18.6 %collective-permute-start.20 = (bf16[848,128]{1,0:T(8,128)(2,1)S(1)}, bf16[848,128]{1,0:T(8,128)(2,1)S(1)}, u32[]{:S(2)}, u32[]{:S(2)}) collective-permute-start(bf16[848,128]{1,0:T(8,128)(2,1)S(1)} %project_2.3), channel_id=1, source_target_pairs={{0,2},{1,3},{2,0},{3,1},{4,6},{5,7},{6,4},{7,5},{8,10},{9,11},{10,... | collective-permute-start | bytes 651272 | tf_op jit(solution)/shard_map/ppermute | solution.py:504
  82.2 18.6 %collective-permute-start.21 = (bf16[848,128]{1,0:T(8,128)(2,1)S(1)}, bf16[848,128]{1,0:T(8,128)(2,1)S(1)}, u32[]{:S(2)}, u32[]{:S(2)}) collective-permute-start(bf16[848,128]{1,0:T(8,128)(2,1)S(1)} %project_1.2), channel_id=1, source_target_pairs={{0,1},{1,0},{2,3},{3,2},{4,5},{5,4},{6,7},{7,6},{8,9},{9,8},{10,11... | collective-permute-start | bytes 651272 | tf_op jit(solution)/shard_map/ppermute | solution.py:504
